TPU v7x, 32 devices: a whole 2x2x4 slice. The times are simulated.
32 devices in a mesh: groups: 2 (over y), tensor: 4 (over z), dp: 4 (over x, core).
Axes of the slice: x: 2, y: 2, z: 4, core: 2. Of those that a mesh axis runs over, the one named last changes fastest.
Arguments:
- acts: bfloat16 [8, 288, 4096], P(('groups', 'dp')), parts along dimension 0, may hold values from -6 to 6
- out_grads: bfloat16 [8, 288, 14336], P(('groups', 'dp'), None, 'tensor'), parts along dimension 0, may hold values from -0.29882812 to 0.29882812
- basis_in: bfloat16 [8192, 4096], P(('groups', 'dp'), 'tensor'), parts along dimension 0, may hold values from -0.09375 to 0.09375
- basis_out: bfloat16 [28672, 14336], P(('groups', 'dp'), 'tensor'), parts along dimension 0, may hold values from -0.046875 to 0.046875
- lengths: int32 [8], P(('groups', 'dp')), parts along dimension 0, may hold values from 96 to 288
Outputs:
- corrections: bfloat16 [28672, 4096], P(('groups', 'tensor'), 'dp'), parts along dimension 0
There are 2 independent parts, one for each index of `groups`. A program takes and returns all parts, laid end to end along the dimension named above; each array names one. Nothing has to cross between parts.
All inputs are finite; a program needn't handle non-finite values.
Results may differ from a plain program's by a relative error of at most 0.0085.
Values may be sent and summed in bfloat16 or wider, within the bound.
No kernel may reach another device: no remote copies, remote signals or barrier semaphores. Data moves between devices by JAX's collectives and lax.ppermute only.
A program may use at most 320 MiB of HBM per device.

v0:
```python
import functools

import jax
import jax.numpy as jnp
from jax import lax
from jax.experimental import pallas as pl
from jax.experimental.pallas import tpu as pltpu
from jax.sharding import PartitionSpec as P

F32 = jnp.float32
BF16 = jnp.bfloat16
MIN_LEN = 96
ALIGN = 16
TILE = 256
STEPS = 4


def square_kernel(start_ref, out_ref, in_ref, c_ref):
    total = None
    for n in range(in_ref.shape[0]):
        rows = pl.ds(pl.multiple_of(start_ref[n], ALIGN), in_ref.shape[1])
        proj = lax.dot_general(out_ref[rows, :], in_ref[n], (((0,), (0,)), ((), ())), preferred_element_type=F32)
        total = proj * proj if total is None else total + proj * proj
    c_ref[...] = total.astype(c_ref.dtype)


def squares(starts, out_proj, in_proj):
    tokens, cols = out_proj.shape
    n, seq, ins = in_proj.shape
    tile = cols
    for t in (512, 256, 128):
        if cols % t == 0:
            tile = t
            break
    return pl.pallas_call(
        square_kernel,
        grid_spec=pltpu.PrefetchScalarGridSpec(
            num_scalar_prefetch=1,
            grid=(cols // tile,),
            in_specs=[
                pl.BlockSpec((tokens, tile), lambda i, s: (0, i)),
                pl.BlockSpec((n, seq, ins), lambda i, s: (0, 0, 0)),
            ],
            out_specs=pl.BlockSpec((tile, ins), lambda i, s: (i, 0)),
        ),
        out_shape=jax.ShapeDtypeStruct((cols, ins), BF16),
        compiler_params=pltpu.CompilerParams(vmem_limit_bytes=60 * 2**20),
        cost_estimate=pl.CostEstimate(
            flops=2 * n * seq * cols * ins, bytes_accessed=2 * (n * seq * (cols + ins) + cols * ins), transcendentals=0
        ),
    )(starts, out_proj, in_proj)


def product_kernel(c_ref, mine_ref, other_ref, b_mine_ref, b_other_ref, given_ref, held_ref):
    i = pl.program_id(0)
    total = jnp.dot(mine_ref[...], b_mine_ref[...], preferred_element_type=F32)
    total = total + jnp.dot(other_ref[...], b_other_ref[...], preferred_element_type=F32)

    @pl.when(i < pl.num_programs(0) // 2)
    def _():
        given_ref[...] = total.astype(given_ref.dtype)

    @pl.when(i >= pl.num_programs(0) // 2)
    def _():
        held_ref[...] = total


def products(c, mine, other, basis):
    rows, depth = mine.shape
    cols = basis.shape[1] // 2
    tile = 896 if cols % 896 == 0 else TILE
    per = cols // tile
    at = lambda i, c: jnp.where(i < per, (1 - c[0]) * per + i, c[0] * per + i - per)
    return pl.pallas_call(
        product_kernel,
        grid_spec=pltpu.PrefetchScalarGridSpec(
            num_scalar_prefetch=1,
            grid=(2 * per,),
            in_specs=[
                pl.BlockSpec((rows, depth), lambda i, c: (0, 0)),
                pl.BlockSpec((rows, depth), lambda i, c: (0, 0)),
                pl.BlockSpec((depth, tile), lambda i, c: (c[0], at(i, c))),
                pl.BlockSpec((depth, tile), lambda i, c: (1 - c[0], at(i, c))),
            ],
            out_specs=[
                pl.BlockSpec((rows, tile), lambda i, c: (0, jnp.minimum(i, per - 1))),
                pl.BlockSpec((rows, tile), lambda i, c: (0, jnp.maximum(i - per, 0))),
            ],
        ),
        out_shape=[jax.ShapeDtypeStruct((rows, cols), BF16), jax.ShapeDtypeStruct((rows, cols), F32)],
        compiler_params=pltpu.CompilerParams(vmem_limit_bytes=36 * 2**20),
        cost_estimate=pl.CostEstimate(flops=1, bytes_accessed=1, transcendentals=0),
    )(c.reshape(1), mine, other, basis, basis)


def places(cap, lens):
    al = [(v + ALIGN - 1) // ALIGN * ALIGN for v in lens]
    return [jnp.int32(0), al[0], cap - al[3] - al[2], cap - al[3]], al


def choose(me, values):
    out = values[0]
    for k in range(1, len(values)):
        out = jnp.where(me == k, values[k], out)
    return out


def pack_kernel(cap, lens_ref, me_ref, own_ref, next_ref, *outs):
    me = me_ref[0]
    lens = [lens_ref[k] for k in range(4)]
    off = places(cap, lens)[0]
    seq = own_ref.shape[0]
    u = cap // STEPS
    for i in range(len(outs) if len(outs) > 1 else outs[0].shape[0]):
        first = jnp.where(me < 2, i, STEPS - 1 - i) * u
        row = first + lax.broadcasted_iota(jnp.int32, (u, seq), 0)
        s = lax.broadcasted_iota(jnp.int32, (u, seq), 1)
        total = None
        for n, ref in ((me, own_ref), (me ^ 1, next_ref)):
            hit = (row == s + choose(n, off)) & (s < choose(n, lens))
            t = jnp.dot(jnp.where(hit, 1.0, 0.0).astype(BF16), ref[...], preferred_element_type=F32)
            total = t if total is None else total + t
        if len(outs) > 1:
            outs[i][...] = total.astype(BF16)
        else:
            outs[0][i] = total.astype(BF16)


def packs(cap, count, split, lens, me, own, following):
    u, width = cap // STEPS, own.shape[1]
    if split and count > 1:
        shapes = [jax.ShapeDtypeStruct((u, width), BF16)] * count
    else:
        shapes = [jax.ShapeDtypeStruct((count, u, width), BF16)]
    out = pl.pallas_call(
        functools.partial(pack_kernel, cap),
        in_specs=[pl.BlockSpec(memory_space=pltpu.SMEM)] * 2 + [pl.BlockSpec(memory_space=pltpu.VMEM)] * 2,
        out_specs=[pl.BlockSpec(memory_space=pltpu.VMEM)] * len(shapes),
        out_shape=shapes,
        compiler_params=pltpu.CompilerParams(vmem_limit_bytes=24 * 2**20),
        cost_estimate=pl.CostEstimate(flops=1, bytes_accessed=1, transcendentals=0),
    )(lens, me.reshape(1), own, following)
    return out if split else out[0]


def pieces_kernel(cap, pairs, first, lens_ref, me_ref, *refs):
    parts = refs[:pairs]
    u = cap // STEPS
    lens = [lens_ref[k] for k in range(4)]
    off, al = places(cap, lens)
    if first:
        mine_ref, other_ref, out_ref, wins, held, rows_in = refs[pairs:]
    else:
        wins, _, out_ref, held = refs[pairs:]
    seq = wins.shape[1]
    starts = [off[0], off[1], off[2] + al[2] - seq, off[3] + al[3] - seq]

    if first:

        @pl.when(pl.program_id(0) == 0)
        def _():
            me = me_ref[0]
            c, hc = me % 2, mine_ref.shape[1]
            for p in range(STEPS):
                at = pl.ds(pl.multiple_of(jnp.where(me < 2, p, STEPS - 1 - p) * u, ALIGN), u)
                rows_in[at, pl.ds(pl.multiple_of(c * hc, 128), hc)] = mine_ref[p * u : (p + 1) * u, :]
                rows_in[at, pl.ds(pl.multiple_of((1 - c) * hc, 128), hc)] = other_ref[p * u : (p + 1) * u, :]
            for n in range(4):
                win = rows_in[pl.ds(pl.multiple_of(starts[n], ALIGN), seq), :]
                row = starts[n] + lax.broadcasted_iota(jnp.int32, win.shape, 0)
                valid = (row >= off[n]) & (row < off[n] + lens[n])
                wins[n] = jnp.where(valid, win.astype(F32), 0.0).astype(BF16)

    for j, part in enumerate(parts):
        held[j * u : (j + 1) * u, :] = part[0]
        k = 2 * pairs - 1 - j
        held[k * u : (k + 1) * u, :] = part[1]

    total = None
    for n in range(4):
        at = pl.ds(pl.multiple_of(starts[n], ALIGN), seq)
        proj = lax.dot_general(held[at, :], wins[n], (((0,), (0,)), ((), ())), preferred_element_type=F32)
        total = proj * proj if total is None else total + proj * proj
    out_ref[...] = total.astype(out_ref.dtype)


def squares_of_pieces(cap, lens, me, parts, in_halves, seq, before=None):
    first = before is None
    pairs = len(parts)
    u, cols = parts[0].shape[1:]
    ins = 2 * in_halves[0].shape[1] if first else before[0].shape[1]
    tile = TILE
    per = cols // tile
    side = 0 if first else 1
    at = lambda i, lens, me: ((me[0] % 2 ^ side) * per + i, 0)
    wins = pl.BlockSpec((4, seq, ins), lambda i, lens, me: (0, 0, 0))
    if first:
        more = [pl.BlockSpec((cap, ins // 2), lambda i, lens, me: (0, 0))] * 2
    else:
        more = [wins, pl.BlockSpec(memory_space=pl.ANY)]
        in_halves = [before[1], before[0]]
    result = jax.ShapeDtypeStruct((2 * cols, ins), BF16)
    out = pl.pallas_call(
        functools.partial(pieces_kernel, cap, pairs, first),
        grid_spec=pltpu.PrefetchScalarGridSpec(
            num_scalar_prefetch=2,
            grid=(per,),
            in_specs=[pl.BlockSpec((2, u, tile), lambda i, lens, me: (0, 0, i))] * pairs + more,
            out_specs=[pl.BlockSpec((tile, ins), at)] + ([wins] if first else []),
            scratch_shapes=[pltpu.VMEM((cap, tile), BF16)] + ([pltpu.VMEM((cap, ins), BF16)] if first else []),
        ),
        out_shape=[result] + ([jax.ShapeDtypeStruct((4, seq, ins), BF16)] if first else []),
        input_output_aliases={} if first else {pairs + 3: 0},
        compiler_params=pltpu.CompilerParams(vmem_limit_bytes=36 * 2**20),
        cost_estimate=pl.CostEstimate(flops=1, bytes_accessed=1, transcendentals=0),
    )(lens, me.reshape(1), *parts, *in_halves)
    return out if first else out[0]


def swap_dp(x, k, n_dp):
    return lax.ppermute(x, "dp", [(d, d ^ k) for d in range(n_dp)])


def project_in(kept, blocks, me):
    rows = blocks[0].shape[0]
    total = None
    for k, b in enumerate(blocks):
        a = lax.dynamic_slice_in_dim(kept, (me ^ k) * rows, rows, axis=1)
        t = jnp.dot(a, b, preferred_element_type=F32)
        total = t if total is None else total + t
    return total.astype(BF16)


def mask_acts(acts, lengths):
    keep = (jnp.arange(acts.shape[1], dtype=jnp.int32)[None, :] < lengths[:, None]).astype(acts.dtype)
    return (acts * keep[:, :, None])[0]


def general(n_dp, acts, out_grads, basis_in, basis_out, lengths):
    seq = acts.shape[1]
    me = lax.axis_index("dp")
    kept = mask_acts(acts, lengths)

    def exchange(x, width):
        parts = [lax.dynamic_slice_in_dim(x, (me ^ k) * width, width, axis=1) for k in range(n_dp)]
        return [parts[0]] + [swap_dp(parts[k], k, n_dp) for k in range(1, n_dp)]

    far = swap_dp(basis_in, 2, n_dp)
    blocks = [basis_in, swap_dp(basis_in, 1, n_dp), far, swap_dp(far, 1, n_dp)]
    in_local = project_in(kept, blocks, me)
    n_chunks = 3
    step = seq // n_chunks
    outs = []
    for j in range(n_chunks):
        g = out_grads[0, j * step : (j + 1) * step]
        whole = lax.all_gather(g, "tensor", axis=1, tiled=True)
        mine = jnp.concatenate(exchange(whole, whole.shape[1] // n_dp), axis=0)
        part = jnp.dot(mine, basis_out, preferred_element_type=F32)
        part = part.reshape(n_dp, step, -1)
        odd = swap_dp(part[1::2].astype(BF16), 1, n_dp)
        s0 = part[0] + odd[0].astype(F32)
        s2 = part[2] + odd[1].astype(F32)
        far = swap_dp(jnp.stack([s2, s0]).astype(BF16), 2, n_dp)
        even = jnp.stack([s0 + far[0].astype(F32), s2 + far[1].astype(F32)]).astype(BF16)
        rest = swap_dp(even, 1, n_dp)
        outs.append(jnp.stack([even[0], rest[0], even[1], rest[1]]))
    in_all = lax.all_gather(in_local, "tensor", axis=1, tiled=True)
    in_proj = jnp.stack(exchange(in_all, in_all.shape[1] // n_dp))
    out_proj = jnp.concatenate(outs, axis=1).reshape(n_dp * seq, -1)
    return squares(jnp.arange(n_dp, dtype=jnp.int32) * seq, out_proj, in_proj)


def home_pairs(hops, across=False):
    pairs = []
    for x in (0, 1):
        for c in (0, 1):
            d = 2 * x + c
            for w0, w1 in hops:
                z0, z1 = (w0, w1) if x == 0 else (3 - w0, 3 - w1)
                if across:
                    pairs.append((z0 * 4 + (d ^ 2), z1 * 4 + d))
                else:
                    pairs.append((z0 * 4 + d, z1 * 4 + d))
    return pairs


def send(x, hops, across=False):
    return lax.ppermute(x, ("tensor", "dp"), home_pairs(hops, across))


def to_home(x):
    return send(x, [(0, 0), (1, 1)], True)


def tie(v, *after):
    return lax.optimization_barrier((v,) + after)[0]


def swap(v, k=1):
    return swap_dp(v, k, 4)


def compact(cap, acts, grads, following, basis_in, basis_out, lens):
    seq = acts.shape[1]
    me = lax.axis_index("dp")
    z = lax.axis_index("tensor")
    x, c = me // 2, me % 2
    w = jnp.where(x == 0, z, 3 - z)
    m = STEPS
    u = cap // m
    c2 = min(m, -(-min(2 * seq, cap - 2 * MIN_LEN) // u))
    want_outer = c == x
    kept = mask_acts(acts, lax.dynamic_slice_in_dim(lens, me, 1))

    def pack(a, b, split):
        return packs(cap, c2, split, lens, me, a, b)

    def merged(own, others, i):
        t = None
        if i < c2:
            t = own[i]
        if m - 1 - i < c2:
            o = others[m - 1 - i]
            t = o if t is None else t + o
        return t

    def halves(outer, inner):
        mine = jnp.where(want_outer, outer, inner)
        return mine, swap(jnp.where(want_outer, inner, outer))

    packed = pack(grads, following, True)
    arrived = [None] * c2
    for i in range(c2 - 1, -1, -1):
        arrived[i] = to_home(packed[i] if i >= c2 - 2 else tie(packed[i], arrived[c2 - 1]))
    far_in = swap(tie(basis_in, arrived[c2 - 1]), 2)
    near_in = swap(tie(basis_in, arrived[c2 - 1]))
    far_near = swap(far_in)

    blocks, given, held, sums, fars = ([None] * m for _ in range(5))
    own, fa, fb, m1 = [None] * m, [None] * (m + 1), [None] * m, [None] * m

    def meet(i):
        outer = jnp.where(w == 0, own[i], jnp.where(w == 1, fa[i], jnp.where(w == 2, fb[i], fa[i + 1])))
        inner = jnp.where(w == 0, m1[i], jnp.where(w == 1, own[i], jnp.where(w == 2, fa[i], fb[i])))
        blocks[i] = halves(outer, inner)

    def product(i):
        mine, other = blocks[i]
        if i >= 1:
            mine = tie(mine, sums[i - 1])
        given[i], held[i] = products(c, mine, other, basis_out)

    def add_core(i):
        sums[i] = held[i] + swap(given[i]).astype(F32)
        fars[i] = swap(sums[i].astype(BF16), 2)

    in_local = None
    for i in range(m):
        own[i] = merged(packed, arrived, i)
        v = own[i] if i == 0 else jnp.where(w == 2, fb[i - 1], own[i])
        after = []
        if i >= 2:
            after += blocks[i - 2]
        if i >= 3:
            after.append(sums[i - 3])
        fa[i] = send(tie(v, *after), [(0, 1), (1, 2)] + ([(2, 3)] if i else []))
        m1[i] = send(own[i], [(1, 0)])
        if i >= 2:
            blocks[i - 2] = (tie(blocks[i - 2][0], fb[i - 1]), blocks[i - 2][1])
            product(i - 2)
            add_core(i - 2)
        if i >= 1:
            meet(i - 1)
        after = []
        if i >= 2:
            after.append(held[i - 2])
        if i >= 3:
            after.append(fars[i - 3])
        if i == m - 1:
            in_local = project_in(kept, [basis_in, near_in, far_in, far_near], me)
            after.append(in_local)
        fb[i] = send(tie(fa[i], *after), [(1, 2), (2, 3)])

    hc = in_local.shape[1] // 2
    in_mine = lax.dynamic_slice_in_dim(in_local, c * hc, hc, axis=1)
    in_given = lax.dynamic_slice_in_dim(in_local, (1 - c) * hc, hc, axis=1)
    in_packed = pack(in_mine, swap(in_given), False)
    in_arrived = to_home(in_packed)
    in_own = jnp.concatenate([merged(in_packed, in_arrived, i) for i in range(m)], axis=0)

    after = [fb[m - 1], sums[m - 3], blocks[m - 2][1]]
    fa[m] = send(tie(fb[m - 1], *after), [(2, 3)])
    r1 = send(tie(in_own, *after), [(0, 1), (1, 2)])
    i1 = send(in_own, [(1, 0)])
    blocks[m - 2] = (tie(blocks[m - 2][0], fb[m - 1]), blocks[m - 2][1])
    product(m - 2)
    add_core(m - 2)
    meet(m - 1)
    r2 = send(tie(r1, fa[m], fars[m - 3], held[m - 2]), [(1, 2), (2, 3)])
    product(m - 1)
    r3 = send(tie(r2, fars[m - 2], held[m - 1]), [(2, 3)])
    add_core(m - 1)
    outer = jnp.where(w == 0, in_own, jnp.where(w == 1, r1, jnp.where(w == 2, r2, r3)))
    inner = jnp.where(w == 0, i1, jnp.where(w == 1, in_own, jnp.where(w == 2, r1, r2)))
    in_mine, in_other = halves(outer, inner)

    mine, rest = [None] * (m // 2), [None] * (m // 2)
    for j in range(m // 2 - 1, -1, -1):
        k = m - 1 - j
        late = tie(fars[k], in_mine, in_other) if j == 0 else fars[k]
        lo = jnp.where(x == 0, sums[j], sums[k]) + jnp.where(x == 0, late, fars[j]).astype(F32)
        hi = jnp.where(x == 0, sums[k], sums[j]) + jnp.where(x == 0, fars[j], late).astype(F32)
        mine[j] = jnp.stack([lo, hi]).astype(BF16)
        rest[j] = swap(mine[j])

    half = squares_of_pieces(cap, lens, me, mine, [in_mine, in_other], seq)
    return squares_of_pieces(cap, lens, me, rest, None, seq, half)


def special(caps, acts, out_grads, basis_in, basis_out, lengths):
    me = lax.axis_index("dp")
    c = me % 2
    every = lax.all_gather(lengths, ("groups", "dp"), axis=0, tiled=True)
    g = out_grads[0]
    half = g.shape[1] // 2
    mine = lax.dynamic_slice_in_dim(g, c * half, half, axis=1)
    given = lax.dynamic_slice_in_dim(g, (1 - c) * half, half, axis=1)
    following = swap_dp(given, 1, 4)
    totals = jnp.sum(((every + ALIGN - 1) // ALIGN * ALIGN).reshape(-1, 4), axis=1)
    need = jnp.max(totals)
    lens = lax.dynamic_slice_in_dim(every, lax.axis_index("groups") * 4, 4)
    index = jnp.int32(0)
    for cap in caps[:-1]:
        index = index + (need > cap).astype(jnp.int32)
    branches = [functools.partial(compact, cap) for cap in caps]
    return lax.switch(index, branches, acts, mine, following, basis_in, basis_out, lens)


def per_device(sizes, caps, acts, out_grads, basis_in, basis_out, lengths):
    if sizes == (4, 4):
        return special(caps, acts, out_grads, basis_in, basis_out, lengths)
    return general(sizes[1], acts, out_grads, basis_in, basis_out, lengths)


CAPS = (768, 832, 896, 960, 1152)


def solution(mesh):
    in_specs = (
        P(("groups", "dp"), None, None),
        P(("groups", "dp"), None, "tensor"),
        P(("groups", "dp"), "tensor"),
        P(("groups", "dp"), "tensor"),
        P(("groups", "dp")),
    )
    out_specs = P(("groups", "tensor"), "dp")
    sizes = (mesh.shape["tensor"], mesh.shape["dp"])
    return jax.shard_map(
        functools.partial(per_device, sizes, CAPS), mesh=mesh, in_specs=in_specs, out_specs=out_specs, check_vma=False
    )
```

profile of v0, /device:TPU:3, one launch (start us, length us, event | category | flops | bytes accessed | tf_op | source)
XLA Modules:
  0.0 340.3 jit_solution(3599827117811397231)
XLA Ops:
  5.2 5.4 %all-reduce = s32[8]{0:T(128)S(1)} all-reduce(s32[8]{0:T(128)S(1)} %dynamic-update-slice), channel_id=1, replica_groups=mesh['groups'=2,'tensor'=4,'dp'=4] {'groups','dp'}, use_global_device_ids=true, to_apply=%add | all-reduce | flops 8 | bytes 64
  14.2 325.1 %conditional.1 = (bf16[3584,1024]{1,0:T(8,128)(2,1)}) conditional(s32[]{:T(128)} %clamp.3, (s32[8]{0:T(128)S(1)}, bf16[1,288,3584]{2,1,0:T(8,128)(2,1)S(1)}, bf16[288,1792]{1,0:T(8,128)(2,1)S(1)}, bf16[3584,3584]{1,0:T(8,128)(2,1)}, bf16[1,288,4096]{2,1,0:T(8,128)(2,1)}, /*index=5*/bf16[1024,1024]{1,0:T(8,128)(2,1)}, ...), branch_computations={%region_2.3_spmd, %region_3.4_spmd, %region_4.5_spmd, %region_5.6_... | conditional | flops 2470109696 | bytes 404393312 | solution.py:436
  36.1 4.1 %branch_3_fun.8 = (bf16[240,1792]{1,0:T(8,128)(2,1)S(1)}, bf16[240,1792]{1,0:T(8,128)(2,1)S(1)}, bf16[240,1792]{1,0:T(8,128)(2,1)S(1)}) custom-call(s32[4]{0:T(128)S(1)} %dynamic_slice.166.lens_ref, s32[1]{0:T(128)} %bitcast.48.me_ref, bf16[288,1792]{1,0:T(8,128)(2,1)S(1)} %dynamic-slice_bitcast_fusion.3.own_ref, bf16[288,1792]{1,0:T(8,128)(2,1)} %copy-done.13), custom_call_target="tpu_custom_call" | custom-call | flops 1 | bytes 1 | tf_op jit(solution)/shard_map/cond/branch_3_fun/pallas_call | solution.py:135
  41.8 6.6 %collective-permute-start.122 = (bf16[240,1792]{1,0:T(8,128)(2,1)S(1)}, bf16[240,1792]{1,0:T(8,128)(2,1)}, u32[]{:S(2)}, u32[]{:S(2)}) collective-permute-start(bf16[240,1792]{1,0:T(8,128)(2,1)S(1)} %get-tuple-element.184), channel_id=1, source_target_pairs={{2,0},{6,4},{3,1},{7,5},{12,14},{8,10},{13,15},{9,11},{18,16},{22,... | collective-permute-start | bytes 2580488 | tf_op jit(solution)/shard_map/cond/branch_3_fun/ppermute | solution.py:288
  49.7 14.1 %collective-permute-done.122 = bf16[240,1792]{1,0:T(8,128)(2,1)} collective-permute-done((bf16[240,1792]{1,0:T(8,128)(2,1)S(1)}, bf16[240,1792]{1,0:T(8,128)(2,1)}, u32[]{:S(2)}, u32[]{:S(2)}) %collective-permute-start.122) | collective-permute-done | bytes 860192 | tf_op jit(solution)/shard_map/cond/branch_3_fun/ppermute | solution.py:288
  63.7 16.9 %collective-permute-done.121 = bf16[240,1792]{1,0:T(8,128)(2,1)S(1)} collective-permute-done((bf16[240,1792]{1,0:T(8,128)(2,1)}, bf16[240,1792]{1,0:T(8,128)(2,1)S(1)}, u32[]{:S(2)}, u32[]{:S(2)}) %collective-permute-start.121) | collective-permute-done | bytes 860192 | tf_op jit(solution)/shard_map/cond/branch_3_fun/ppermute | solution.py:288
  80.7 2.8 broadcast_select_fusion.43
  86.4 5.3 %collective-permute-start.129 = (bf16[240,1792]{1,0:T(8,128)(2,1)S(1)}, bf16[240,1792]{1,0:T(8,128)(2,1)}, u32[]{:S(2)}, u32[]{:S(2)}) collective-permute-start(bf16[240,1792]{1,0:T(8,128)(2,1)S(1)} %get-tuple-element.183), channel_id=1, source_target_pairs={{2,0},{6,4},{3,1},{7,5},{12,14},{8,10},{13,15},{9,11},{18,16},{22,... | collective-permute-start | bytes 2580488 | tf_op jit(solution)/shard_map/cond/branch_3_fun/ppermute | solution.py:288
  93.6 9.0 %collective-permute-done.123 = bf16[240,1792]{1,0:T(8,128)(2,1)S(1)} collective-permute-done((bf16[240,1792]{1,0:T(8,128)(2,1)}, bf16[240,1792]{1,0:T(8,128)(2,1)S(1)}, u32[]{:S(2)}, u32[]{:S(2)}) %collective-permute-start.123) | collective-permute-done | bytes 860192 | tf_op jit(solution)/shard_map/cond/branch_3_fun/ppermute | solution.py:288
  105.6 4.6 %collective-permute-start.126 = (bf16[240,1792]{1,0:T(8,128)(2,1)S(1)}, bf16[240,1792]{1,0:T(8,128)(2,1)S(1)}, u32[]{:S(2)}, u32[]{:S(2)}) collective-permute-start(bf16[240,1792]{1,0:T(8,128)(2,1)S(1)} %get-tuple-element.495), channel_id=1, source_target_pairs={{0,1},{1,0},{2,3},{3,2},{4,5},{5,4},{6,7},{7,6},{8,9},{9,8},{10,11... | collective-permute-start | bytes 2580488 | tf_op jit(solution)/shard_map/cond/branch_3_fun/ppermute | solution.py:221
  110.3 10.3 %collective-permute-done.125 = bf16[240,1792]{1,0:T(8,128)(2,1)S(1)} collective-permute-done((bf16[240,1792]{1,0:T(8,128)(2,1)S(1)}, bf16[240,1792]{1,0:T(8,128)(2,1)S(1)}, u32[]{:S(2)}, u32[]{:S(2)}) %collective-permute-start.125) | collective-permute-done | bytes 860192 | tf_op jit(solution)/shard_map/cond/branch_3_fun/ppermute | solution.py:288
  123.5 12.4 %branch_3_fun.9 = (bf16[240,1792]{1,0:T(8,128)(2,1)S(1)}, f32[240,1792]{1,0:T(8,128)S(1)}) custom-call(s32[1]{0:T(128)} %bitcast.49.c_ref, bf16[240,1792]{1,0:T(8,128)(2,1)S(1)} %broadcast_select_fusion.51.mine_ref, bf16[240,1792]{1,0:T(8,128)(2,1)S(1)} %collective-permute-done.126.other_ref, bf16[3584,3584]{1,0:T(8,128)(2,1)} %get-tuple-element.313.b_mine_ref.b_other_ref, ...), custom_call_target="tpu_custom_call" | custom-call | flops 1 | bytes 1 | tf_op jit(solution)/shard_map/cond/branch_3_fun/pallas_call | solution.py:74
  135.9 5.5 %collective-permute-start.127 = (bf16[240,1792]{1,0:T(8,128)(2,1)S(1)}, bf16[240,1792]{1,0:T(8,128)(2,1)S(1)}, u32[]{:S(2)}, u32[]{:S(2)}) collective-permute-start(bf16[240,1792]{1,0:T(8,128)(2,1)S(1)} %get-tuple-element.188), channel_id=1, source_target_pairs={{0,1},{1,0},{2,3},{3,2},{4,5},{5,4},{6,7},{7,6},{8,9},{9,8},{10,11... | collective-permute-start | bytes 2580488 | tf_op jit(solution)/shard_map/cond/branch_3_fun/ppermute | solution.py:221
  142.3 4.9 %collective-permute-start.128 = (bf16[240,1792]{1,0:T(8,128)(2,1)S(1)}, bf16[240,1792]{1,0:T(8,128)(2,1)S(1)}, u32[]{:S(2)}, u32[]{:S(2)}) collective-permute-start(bf16[240,1792]{1,0:T(8,128)(2,1)S(1)} %get-tuple-element.189), channel_id=1, source_target_pairs={{2,0},{6,4},{3,1},{7,5},{12,14},{8,10},{13,15},{9,11},{18,16},{22,... | collective-permute-start | bytes 2580488 | tf_op jit(solution)/shard_map/cond/branch_3_fun/ppermute | solution.py:288
  147.2 3.1 collective-permute-done.137
  150.3 9.2 %collective-permute-start.138 = (bf16[1024,1024]{1,0:T(8,128)(2,1)S(1)}, bf16[1024,1024]{1,0:T(8,128)(2,1)S(1)}, u32[]{:S(2)}, u32[]{:S(2)}) collective-permute-start(bf16[1024,1024]{1,0:T(8,128)(2,1)S(1)} %collective-permute-done.137), channel_id=1, source_target_pairs={{0,1},{1,0},{2,3},{3,2},{4,5},{5,4},{6,7},{7,6},{8,9},{9,8},{10,11... | collective-permute-start | bytes 6291464 | tf_op jit(solution)/shard_map/cond/branch_3_fun/ppermute | solution.py:221
  161.6 7.1 %collective-permute-done.128 = bf16[240,1792]{1,0:T(8,128)(2,1)S(1)} collective-permute-done((bf16[240,1792]{1,0:T(8,128)(2,1)S(1)}, bf16[240,1792]{1,0:T(8,128)(2,1)S(1)}, u32[]{:S(2)}, u32[]{:S(2)}) %collective-permute-start.128) | collective-permute-done | bytes 860192 | tf_op jit(solution)/shard_map/cond/branch_3_fun/ppermute | solution.py:288
  169.3 14.9 %collective-permute-done.131 = bf16[240,1792]{1,0:T(8,128)(2,1)S(1)} collective-permute-done((bf16[240,1792]{1,0:T(8,128)(2,1)S(1)}, bf16[240,1792]{1,0:T(8,128)(2,1)S(1)}, u32[]{:S(2)}, u32[]{:S(2)}) %collective-permute-start.131) | collective-permute-done | bytes 860192 | tf_op jit(solution)/shard_map/cond/branch_3_fun/ppermute | solution.py:288
  191.4 12.3 %branch_3_fun.10 = (bf16[240,1792]{1,0:T(8,128)(2,1)S(1)}, f32[240,1792]{1,0:T(8,128)S(1)}) custom-call(s32[1]{0:T(128)} %bitcast.49.c_ref, bf16[240,1792]{1,0:T(8,128)(2,1)S(1)} %broadcast_select_fusion.49.mine_ref, bf16[240,1792]{1,0:T(8,128)(2,1)S(1)} %collective-permute-done.133.other_ref, bf16[3584,3584]{1,0:T(8,128)(2,1)} %get-tuple-element.313.b_mine_ref.b_other_ref, ...), custom_call_target="tpu_custom_call" | custom-call | flops 1 | bytes 1 | tf_op jit(solution)/shard_map/cond/branch_3_fun/pallas_call | solution.py:74
  213.3 16.2 %collective-permute-done.139 = bf16[240,1792]{1,0:T(8,128)(2,1)S(1)} collective-permute-done((bf16[240,1792]{1,0:T(8,128)(2,1)S(1)}, bf16[240,1792]{1,0:T(8,128)(2,1)S(1)}, u32[]{:S(2)}, u32[]{:S(2)}) %collective-permute-start.139) | collective-permute-done | bytes 860192 | tf_op jit(solution)/shard_map/cond/branch_3_fun/ppermute | solution.py:288
  231.8 3.2 collective-permute-start.152
  235.0 12.3 %branch_3_fun.11 = (bf16[240,1792]{1,0:T(8,128)(2,1)S(1)}, f32[240,1792]{1,0:T(8,128)S(1)}) custom-call(s32[1]{0:T(128)} %bitcast.49.c_ref, bf16[240,1792]{1,0:T(8,128)(2,1)S(1)} %get-tuple-element.203.mine_ref, bf16[240,1792]{1,0:T(8,128)(2,1)S(1)} %collective-permute-done.142.other_ref, bf16[3584,3584]{1,0:T(8,128)(2,1)} %get-tuple-element.313.b_mine_ref.b_other_ref, ...), custom_call_target="tpu_custom_call" | custom-call | flops 1 | bytes 1 | tf_op jit(solution)/shard_map/cond/branch_3_fun/pallas_call | solution.py:74
  247.3 3.3 collective-permute-start.145
  250.9 2.5 collective-permute-start.146
  255.4 12.2 %branch_3_fun.12 = (bf16[240,1792]{1,0:T(8,128)(2,1)S(1)}, f32[240,1792]{1,0:T(8,128)S(1)}) custom-call(s32[1]{0:T(128)} %bitcast.49.c_ref, bf16[240,1792]{1,0:T(8,128)(2,1)S(1)} %broadcast_select_fusion.46.mine_ref, bf16[240,1792]{1,0:T(8,128)(2,1)S(1)} %collective-permute-done.146.other_ref, bf16[3584,3584]{1,0:T(8,128)(2,1)} %get-tuple-element.313.b_mine_ref.b_other_ref, ...), custom_call_target="tpu_custom_call" | custom-call | flops 1 | bytes 1 | tf_op jit(solution)/shard_map/cond/branch_3_fun/pallas_call | solution.py:74
  267.6 2.9 collective-permute-start.147
  271.2 2.7 collective-permute-done.154
  273.9 2.7 collective-permute-done.153
  278.5 19.4 %collective-permute-done.155 = bf16[960,512]{1,0:T(8,128)(2,1)S(1)} collective-permute-done((bf16[960,512]{1,0:T(8,128)(2,1)S(1)}, bf16[960,512]{1,0:T(8,128)(2,1)S(1)}, u32[]{:S(2)}, u32[]{:S(2)}) %collective-permute-start.155) | collective-permute-done | bytes 983072 | tf_op jit(solution)/shard_map/cond/branch_3_fun/ppermute | solution.py:288
  298.7 4.9 %collective-permute-start.157 = (bf16[960,512]{1,0:T(8,128)(2,1)S(1)}, bf16[960,512]{1,0:T(8,128)(2,1)S(1)}, u32[]{:S(2)}, u32[]{:S(2)}) collective-permute-start(bf16[960,512]{1,0:T(8,128)(2,1)S(1)} %get-tuple-element.475), channel_id=1, source_target_pairs={{0,1},{1,0},{2,3},{3,2},{4,5},{5,4},{6,7},{7,6},{8,9},{9,8},{10,11... | collective-permute-start | bytes 2949128 | tf_op jit(solution)/shard_map/cond/branch_3_fun/ppermute | solution.py:221
  307.1 11.8 %branch_3_fun.14 = (bf16[3584,1024]{1,0:T(8,128)(2,1)}, bf16[4,288,1024]{2,1,0:T(8,128)(2,1)S(1)}) custom-call(s32[4]{0:T(128)S(1)} %dynamic_slice.166.lens_ref, s32[1]{0:T(128)} %bitcast.48.me_ref, bf16[2,240,1792]{2,1,0:T(8,128)(2,1)S(1)} %pad_maximum_fusion.9.refs_0_, bf16[2,240,1792]{2,1,0:T(8,128)(2,1)S(1)} %pad_maximum_fusion.10.refs_1_, ...), custom_call_target="tpu_custom_call" | custom-call | flops 1 | bytes 1 | tf_op jit(solution)/shard_map/cond/branch_3_fun/pallas_call | solution.py:203
  318.9 10.8 %branch_3_fun.15 = bf16[3584,1024]{1,0:T(8,128)(2,1)} custom-call(s32[4]{0:T(128)S(1)} %dynamic_slice.166.lens_ref, s32[1]{0:T(128)} %bitcast.48.me_ref, bf16[2,240,1792]{2,1,0:T(8,128)(2,1)S(1)} %collective-permute-done.158.refs_0_, bf16[2,240,1792]{2,1,0:T(8,128)(2,1)S(1)} %collective-permute-done.159.refs_1_, ...), custom_call_target="tpu_custom_call", output_to_operand_aliasing={{}: (5, {})} | custom-call | flops 1 | bytes 1 | tf_op jit(solution)/shard_map/cond/branch_3_fun/pallas_call | solution.py:203
  (115 shorter events, 51.7 us)
Async XLA Ops:
  41.8 22.0 %collective-permute-start.122 = (bf16[240,1792]{1,0:T(8,128)(2,1)S(1)}, bf16[240,1792]{1,0:T(8,128)(2,1)}, u32[]{:S(2)}, u32[]{:S(2)}) collective-permute-start(bf16[240,1792]{1,0:T(8,128)(2,1)S(1)} %get-tuple-element.184), channel_id=1, source_target_pairs={{2,0},{6,4},{3,1},{7,5},{12,14},{8,10},{13,15},{9,11},{18,16},{22,... | collective-permute-start | bytes 2580488 | tf_op jit(solution)/shard_map/cond/branch_3_fun/ppermute | solution.py:288
  48.3 32.3 %collective-permute-start.121 = (bf16[240,1792]{1,0:T(8,128)(2,1)}, bf16[240,1792]{1,0:T(8,128)(2,1)S(1)}, u32[]{:S(2)}, u32[]{:S(2)}) collective-permute-start(bf16[240,1792]{1,0:T(8,128)(2,1)} %collective-permute-done.120), channel_id=1, source_target_pairs={{4,8},{8,12},{5,9},{9,13},{10,6},{6,2},{11,7},{7,3},{20,24},{24,28... | collective-permute-start | bytes 2580488 | tf_op jit(solution)/shard_map/cond/branch_3_fun/ppermute | solution.py:288
  83.5 19.1 %collective-permute-start.123 = (bf16[240,1792]{1,0:T(8,128)(2,1)}, bf16[240,1792]{1,0:T(8,128)(2,1)S(1)}, u32[]{:S(2)}, u32[]{:S(2)}) collective-permute-start(bf16[240,1792]{1,0:T(8,128)(2,1)} %get-tuple-element.498), channel_id=1, source_target_pairs={{0,4},{4,8},{8,12},{1,5},{5,9},{9,13},{14,10},{10,6},{6,2},{15,11}... | collective-permute-start | bytes 2580488 | tf_op jit(solution)/shard_map/cond/branch_3_fun/ppermute | solution.py:288
  84.8 19.1 %collective-permute-start.124 = (bf16[240,1792]{1,0:T(8,128)(2,1)S(1)}, bf16[240,1792]{1,0:T(8,128)(2,1)}, u32[]{:S(2)}, u32[]{:S(2)}) collective-permute-start(bf16[240,1792]{1,0:T(8,128)(2,1)S(1)} %get-tuple-element.189), channel_id=1, source_target_pairs={{4,0},{5,1},{10,14},{11,15},{20,16},{21,17},{26,30},{27,31}} | collective-permute-start | bytes 2580488 | tf_op jit(solution)/shard_map/cond/branch_3_fun/ppermute | solution.py:288
  86.4 23.8 %collective-permute-start.129 = (bf16[240,1792]{1,0:T(8,128)(2,1)S(1)}, bf16[240,1792]{1,0:T(8,128)(2,1)}, u32[]{:S(2)}, u32[]{:S(2)}) collective-permute-start(bf16[240,1792]{1,0:T(8,128)(2,1)S(1)} %get-tuple-element.183), channel_id=1, source_target_pairs={{2,0},{6,4},{3,1},{7,5},{12,14},{8,10},{13,15},{9,11},{18,16},{22,... | collective-permute-start | bytes 2580488 | tf_op jit(solution)/shard_map/cond/branch_3_fun/ppermute | solution.py:288
  92.8 57.5 %collective-permute-start.137 = (bf16[1024,1024]{1,0:T(8,128)(2,1)}, bf16[1024,1024]{1,0:T(8,128)(2,1)S(1)}, u32[]{:S(2)}, u32[]{:S(2)}) collective-permute-start(bf16[1024,1024]{1,0:T(8,128)(2,1)} %get-tuple-element.198), channel_id=1, source_target_pairs={{0,2},{1,3},{2,0},{3,1},{4,6},{5,7},{6,4},{7,5},{8,10},{9,11},{10,... | collective-permute-start | bytes 6291464 | tf_op jit(solution)/shard_map/cond/branch_3_fun/ppermute | solution.py:221
  92.8 49.4 %collective-permute-start.132 = (bf16[240,1792]{1,0:T(8,128)(2,1)}, bf16[240,1792]{1,0:T(8,128)(2,1)S(1)}, u32[]{:S(2)}, u32[]{:S(2)}) collective-permute-start(bf16[240,1792]{1,0:T(8,128)(2,1)} %get-tuple-element.499), channel_id=1, source_target_pairs={{4,0},{5,1},{10,14},{11,15},{20,16},{21,17},{26,30},{27,31}} | collective-permute-start | bytes 2580488 | tf_op jit(solution)/shard_map/cond/branch_3_fun/ppermute | solution.py:288
  102.6 18.0 %collective-permute-start.125 = (bf16[240,1792]{1,0:T(8,128)(2,1)S(1)}, bf16[240,1792]{1,0:T(8,128)(2,1)S(1)}, u32[]{:S(2)}, u32[]{:S(2)}) collective-permute-start(bf16[240,1792]{1,0:T(8,128)(2,1)S(1)} %collective-permute-done.123), channel_id=1, source_target_pairs={{4,8},{8,12},{5,9},{9,13},{10,6},{6,2},{11,7},{7,3},{20,24},{24,28... | collective-permute-start | bytes 2580488 | tf_op jit(solution)/shard_map/cond/branch_3_fun/ppermute | solution.py:288
  105.6 16.4 %collective-permute-start.126 = (bf16[240,1792]{1,0:T(8,128)(2,1)S(1)}, bf16[240,1792]{1,0:T(8,128)(2,1)S(1)}, u32[]{:S(2)}, u32[]{:S(2)}) collective-permute-start(bf16[240,1792]{1,0:T(8,128)(2,1)S(1)} %get-tuple-element.495), channel_id=1, source_target_pairs={{0,1},{1,0},{2,3},{3,2},{4,5},{5,4},{6,7},{7,6},{8,9},{9,8},{10,11... | collective-permute-start | bytes 2580488 | tf_op jit(solution)/shard_map/cond/branch_3_fun/ppermute | solution.py:221
  122.0 37.5 %collective-permute-start.130 = (bf16[240,1792]{1,0:T(8,128)(2,1)S(1)}, bf16[240,1792]{1,0:T(8,128)(2,1)S(1)}, u32[]{:S(2)}, u32[]{:S(2)}) collective-permute-start(bf16[240,1792]{1,0:T(8,128)(2,1)S(1)} %get-tuple-element.190), channel_id=1, source_target_pairs={{0,4},{4,8},{8,12},{1,5},{5,9},{9,13},{14,10},{10,6},{6,2},{15,11}... | collective-permute-start | bytes 2580488 | tf_op jit(solution)/shard_map/cond/branch_3_fun/ppermute | solution.py:288
  135.9 24.0 %collective-permute-start.127 = (bf16[240,1792]{1,0:T(8,128)(2,1)S(1)}, bf16[240,1792]{1,0:T(8,128)(2,1)S(1)}, u32[]{:S(2)}, u32[]{:S(2)}) collective-permute-start(bf16[240,1792]{1,0:T(8,128)(2,1)S(1)} %get-tuple-element.188), channel_id=1, source_target_pairs={{0,1},{1,0},{2,3},{3,2},{4,5},{5,4},{6,7},{7,6},{8,9},{9,8},{10,11... | collective-permute-start | bytes 2580488 | tf_op jit(solution)/shard_map/cond/branch_3_fun/ppermute | solution.py:221
  142.2 43.6 %collective-permute-start.136 = (bf16[1024,1024]{1,0:T(8,128)(2,1)S(1)}, bf16[1024,1024]{1,0:T(8,128)(2,1)S(1)}, u32[]{:S(2)}, u32[]{:S(2)}) collective-permute-start(bf16[1024,1024]{1,0:T(8,128)(2,1)S(1)} %copy-done.49), channel_id=1, source_target_pairs={{0,1},{1,0},{2,3},{3,2},{4,5},{5,4},{6,7},{7,6},{8,9},{9,8},{10,11... | collective-permute-start | bytes 6291464 | tf_op jit(solution)/shard_map/cond/branch_3_fun/ppermute | solution.py:221
  142.3 26.3 %collective-permute-start.128 = (bf16[240,1792]{1,0:T(8,128)(2,1)S(1)}, bf16[240,1792]{1,0:T(8,128)(2,1)S(1)}, u32[]{:S(2)}, u32[]{:S(2)}) collective-permute-start(bf16[240,1792]{1,0:T(8,128)(2,1)S(1)} %get-tuple-element.189), channel_id=1, source_target_pairs={{2,0},{6,4},{3,1},{7,5},{12,14},{8,10},{13,15},{9,11},{18,16},{22,... | collective-permute-start | bytes 2580488 | tf_op jit(solution)/shard_map/cond/branch_3_fun/ppermute | solution.py:288
  150.3 38.6 %collective-permute-start.138 = (bf16[1024,1024]{1,0:T(8,128)(2,1)S(1)}, bf16[1024,1024]{1,0:T(8,128)(2,1)S(1)}, u32[]{:S(2)}, u32[]{:S(2)}) collective-permute-start(bf16[1024,1024]{1,0:T(8,128)(2,1)S(1)} %collective-permute-done.137), channel_id=1, source_target_pairs={{0,1},{1,0},{2,3},{3,2},{4,5},{5,4},{6,7},{7,6},{8,9},{9,8},{10,11... | collective-permute-start | bytes 6291464 | tf_op jit(solution)/shard_map/cond/branch_3_fun/ppermute | solution.py:221
  159.8 24.5 %collective-permute-start.133 = (bf16[240,1792]{1,0:T(8,128)(2,1)S(1)}, bf16[240,1792]{1,0:T(8,128)(2,1)S(1)}, u32[]{:S(2)}, u32[]{:S(2)}) collective-permute-start(bf16[240,1792]{1,0:T(8,128)(2,1)S(1)} %get-tuple-element.488), channel_id=1, source_target_pairs={{0,1},{1,0},{2,3},{3,2},{4,5},{5,4},{6,7},{7,6},{8,9},{9,8},{10,11... | collective-permute-start | bytes 2580488 | tf_op jit(solution)/shard_map/cond/branch_3_fun/ppermute | solution.py:221
  159.9 24.3 %collective-permute-start.131 = (bf16[240,1792]{1,0:T(8,128)(2,1)S(1)}, bf16[240,1792]{1,0:T(8,128)(2,1)S(1)}, u32[]{:S(2)}, u32[]{:S(2)}) collective-permute-start(bf16[240,1792]{1,0:T(8,128)(2,1)S(1)} %collective-permute-done.130), channel_id=1, source_target_pairs={{4,8},{8,12},{5,9},{9,13},{10,6},{6,2},{11,7},{7,3},{20,24},{24,28... | collective-permute-start | bytes 2580488 | tf_op jit(solution)/shard_map/cond/branch_3_fun/ppermute | solution.py:288
  168.6 35.2 %collective-permute-start.141 = (bf16[240,1792]{1,0:T(8,128)(2,1)S(1)}, bf16[240,1792]{1,0:T(8,128)(2,1)S(1)}, u32[]{:S(2)}, u32[]{:S(2)}) collective-permute-start(bf16[240,1792]{1,0:T(8,128)(2,1)S(1)} %get-tuple-element.492), channel_id=1, source_target_pairs={{4,0},{5,1},{10,14},{11,15},{20,16},{21,17},{26,30},{27,31}} | collective-permute-start | bytes 2580488 | tf_op jit(solution)/shard_map/cond/branch_3_fun/ppermute | solution.py:288
  184.3 21.5 %collective-permute-start.134 = (bf16[240,1792]{1,0:T(8,128)(2,1)S(1)}, bf16[240,1792]{1,0:T(8,128)(2,1)S(1)}, u32[]{:S(2)}, u32[]{:S(2)}) collective-permute-start(bf16[240,1792]{1,0:T(8,128)(2,1)S(1)} %broadcast_select_fusion.41), channel_id=1, source_target_pairs={{0,4},{4,8},{8,12},{1,5},{5,9},{9,13},{14,10},{10,6},{6,2},{15,11}... | collective-permute-start | bytes 2580488 | tf_op jit(solution)/shard_map/cond/branch_3_fun/ppermute | solution.py:288
  187.4 20.8 %collective-permute-start.135 = (bf16[240,1792]{1,0:T(8,128)(2,1)S(1)}, bf16[240,1792]{1,0:T(8,128)(2,1)S(1)}, u32[]{:S(2)}, u32[]{:S(2)}) collective-permute-start(bf16[240,1792]{1,0:T(8,128)(2,1)S(1)} %get-tuple-element.493), channel_id=1, source_target_pairs={{0,2},{1,3},{2,0},{3,1},{4,6},{5,7},{6,4},{7,5},{8,10},{9,11},{10,... | collective-permute-start | bytes 2580488 | tf_op jit(solution)/shard_map/cond/branch_3_fun/ppermute | solution.py:221
  189.8 19.8 %collective-permute-start.149 = (bf16[288,512]{1,0:T(8,128)(2,1)S(1)}, bf16[288,512]{1,0:T(8,128)(2,1)S(1)}, u32[]{:S(2)}, u32[]{:S(2)}) collective-permute-start(bf16[288,512]{1,0:T(8,128)(2,1)S(1)} %get-tuple-element.559), channel_id=1, source_target_pairs={{0,1},{1,0},{2,3},{3,2},{4,5},{5,4},{6,7},{7,6},{8,9},{9,8},{10,11... | collective-permute-start | bytes 884744 | tf_op jit(solution)/shard_map/cond/branch_3_fun/ppermute | solution.py:221
  208.2 21.3 %collective-permute-start.139 = (bf16[240,1792]{1,0:T(8,128)(2,1)S(1)}, bf16[240,1792]{1,0:T(8,128)(2,1)S(1)}, u32[]{:S(2)}, u32[]{:S(2)}) collective-permute-start(bf16[240,1792]{1,0:T(8,128)(2,1)S(1)} %collective-permute-done.134), channel_id=1, source_target_pairs={{4,8},{8,12},{5,9},{9,13},{10,6},{6,2},{11,7},{7,3},{20,24},{24,28... | collective-permute-start | bytes 2580488 | tf_op jit(solution)/shard_map/cond/branch_3_fun/ppermute | solution.py:288
  211.0 19.8 %collective-permute-start.150 = (bf16[3,240,512]{2,1,0:T(8,128)(2,1)S(1)}, bf16[3,240,512]{2,1,0:T(8,128)(2,1)S(1)}, u32[]{:S(2)}, u32[]{:S(2)}) collective-permute-start(bf16[3,240,512]{2,1,0:T(8,128)(2,1)S(1)} %branch_3_fun.13), channel_id=1, source_target_pairs={{2,0},{6,4},{3,1},{7,5},{12,14},{8,10},{13,15},{9,11},{18,16},{22,... | collective-permute-start | bytes 2211848 | tf_op jit(solution)/shard_map/cond/branch_3_fun/ppermute | solution.py:288
  212.4 38.2 %collective-permute-start.144 = (bf16[240,1792]{1,0:T(8,128)(2,1)S(1)}, bf16[240,1792]{1,0:T(8,128)(2,1)S(1)}, u32[]{:S(2)}, u32[]{:S(2)}) collective-permute-start(bf16[240,1792]{1,0:T(8,128)(2,1)S(1)} %collective-permute-done.128), channel_id=1, source_target_pairs={{4,0},{5,1},{10,14},{11,15},{20,16},{21,17},{26,30},{27,31}} | collective-permute-start | bytes 2580488 | tf_op jit(solution)/shard_map/cond/branch_3_fun/ppermute | solution.py:288
  229.6 21.0 %collective-permute-start.143 = (bf16[240,1792]{1,0:T(8,128)(2,1)S(1)}, bf16[240,1792]{1,0:T(8,128)(2,1)S(1)}, u32[]{:S(2)}, u32[]{:S(2)}) collective-permute-start(bf16[240,1792]{1,0:T(8,128)(2,1)S(1)} %collective-permute-done.139), channel_id=1, source_target_pairs={{8,12},{9,13},{6,2},{7,3},{24,28},{25,29},{22,18},{23,19}} | collective-permute-start | bytes 2580488 | tf_op jit(solution)/shard_map/cond/branch_3_fun/ppermute | solution.py:288
  231.1 22.4 %collective-permute-start.151 = (bf16[960,512]{1,0:T(8,128)(2,1)S(1)}, bf16[960,512]{1,0:T(8,128)(2,1)S(1)}, u32[]{:S(2)}, u32[]{:S(2)}) collective-permute-start(bf16[960,512]{1,0:T(8,128)(2,1)S(1)} %pad_maximum_fusion.11), channel_id=1, source_target_pairs={{0,4},{4,8},{1,5},{5,9},{14,10},{10,6},{15,11},{11,7},{16,20},{20,... | collective-permute-start | bytes 2949128 | tf_op jit(solution)/shard_map/cond/branch_3_fun/ppermute | solution.py:288
  231.8 21.6 %collective-permute-start.152 = (bf16[240,1792]{1,0:T(8,128)(2,1)S(1)}, bf16[240,1792]{1,0:T(8,128)(2,1)S(1)}, u32[]{:S(2)}, u32[]{:S(2)}) collective-permute-start(bf16[240,1792]{1,0:T(8,128)(2,1)S(1)} %get-tuple-element.480), channel_id=1, source_target_pairs={{0,2},{1,3},{2,0},{3,1},{4,6},{5,7},{6,4},{7,5},{8,10},{9,11},{10,... | collective-permute-start | bytes 2580488 | tf_op jit(solution)/shard_map/cond/branch_3_fun/ppermute | solution.py:221
  253.4 23.2 %collective-permute-start.153 = (bf16[960,512]{1,0:T(8,128)(2,1)S(1)}, bf16[960,512]{1,0:T(8,128)(2,1)S(1)}, u32[]{:S(2)}, u32[]{:S(2)}) collective-permute-start(bf16[960,512]{1,0:T(8,128)(2,1)S(1)} %collective-permute-done.151), channel_id=1, source_target_pairs={{4,8},{8,12},{5,9},{9,13},{10,6},{6,2},{11,7},{7,3},{20,24},{24,28... | collective-permute-start | bytes 2949128 | tf_op jit(solution)/shard_map/cond/branch_3_fun/ppermute | solution.py:288
  254.9 19.0 %collective-permute-start.154 = (bf16[240,1792]{1,0:T(8,128)(2,1)S(1)}, bf16[240,1792]{1,0:T(8,128)(2,1)S(1)}, u32[]{:S(2)}, u32[]{:S(2)}) collective-permute-start(bf16[240,1792]{1,0:T(8,128)(2,1)S(1)} %get-tuple-element.478), channel_id=1, source_target_pairs={{0,2},{1,3},{2,0},{3,1},{4,6},{5,7},{6,4},{7,5},{8,10},{9,11},{10,... | collective-permute-start | bytes 2580488 | tf_op jit(solution)/shard_map/cond/branch_3_fun/ppermute | solution.py:221
  276.6 21.2 %collective-permute-start.155 = (bf16[960,512]{1,0:T(8,128)(2,1)S(1)}, bf16[960,512]{1,0:T(8,128)(2,1)S(1)}, u32[]{:S(2)}, u32[]{:S(2)}) collective-permute-start(bf16[960,512]{1,0:T(8,128)(2,1)S(1)} %collective-permute-done.153), channel_id=1, source_target_pairs={{8,12},{9,13},{6,2},{7,3},{24,28},{25,29},{22,18},{23,19}} | collective-permute-start | bytes 2949128 | tf_op jit(solution)/shard_map/cond/branch_3_fun/ppermute | solution.py:288
  278.4 26.2 %collective-permute-start.148 = (bf16[240,1792]{1,0:T(8,128)(2,1)S(1)}, bf16[240,1792]{1,0:T(8,128)(2,1)S(1)}, u32[]{:S(2)}, u32[]{:S(2)}) collective-permute-start(bf16[240,1792]{1,0:T(8,128)(2,1)S(1)} %fusion.71), channel_id=1, source_target_pairs={{0,2},{1,3},{2,0},{3,1},{4,6},{5,7},{6,4},{7,5},{8,10},{9,11},{10,... | collective-permute-start | bytes 2580488 | tf_op jit(solution)/shard_map/cond/branch_3_fun/ppermute | solution.py:221
  304.4 14.6 %collective-permute-start.159 = (bf16[2,240,1792]{2,1,0:T(8,128)(2,1)S(1)}, bf16[2,240,1792]{2,1,0:T(8,128)(2,1)S(1)}, u32[]{:S(2)}, u32[]{:S(2)}) collective-permute-start(bf16[2,240,1792]{2,1,0:T(8,128)(2,1)S(1)} %pad_maximum_fusion.10.refs_1_), channel_id=1, source_target_pairs={{0,1},{1,0},{2,3},{3,2},{4,5},{5,4},{6,7},{7,6},{8,9},{9,8},{10,11... | collective-permute-start | bytes 5160968 | tf_op jit(solution)/shard_map/cond/branch_3_fun/ppermute | solution.py:221
  306.7 12.3 %collective-permute-start.158 = (bf16[2,240,1792]{2,1,0:T(8,128)(2,1)S(1)}, bf16[2,240,1792]{2,1,0:T(8,128)(2,1)S(1)}, u32[]{:S(2)}, u32[]{:S(2)}) collective-permute-start(bf16[2,240,1792]{2,1,0:T(8,128)(2,1)S(1)} %pad_maximum_fusion.9.refs_0_), channel_id=1, source_target_pairs={{0,1},{1,0},{2,3},{3,2},{4,5},{5,4},{6,7},{7,6},{8,9},{9,8},{10,11... | collective-permute-start | bytes 5160968 | tf_op jit(solution)/shard_map/cond/branch_3_fun/ppermute | solution.py:221
  (16 other events, 150.2 us)
where the time goes:
time: 345 us; the launch traced here: 340 us
  waiting for transfers between devices  120 us (35%)
  starting transfers between devices  81 us (23%)
  Pallas kernels  77.4 us (22%)
  loops' own time  31 us (9%)
  other arithmetic  12.5 us (4%)
  local copies, waits for them, and re-layouts  5.48 us (2%)
  blocking collectives  5.36 us (2%)
  between operations  4.46 us (1%)
    ppermute x21, waiting for transfers between devices, send(): return lax.ppermute(x, ('tensor', 'dp'), home_pairs(hops, across))  113 us
    pallas_call x4, Pallas kernels, products(): pl.pallas_call(product_kernel, grid_spec=pltpu.PrefetchScalarGridSpec(num...  49.1 us
    ppermute x20, starting transfers between devices, swap_dp(): return lax.ppermute(x, 'dp', [(d, d ^ k) for d in range(n_dp)])  42.9 us
    ppermute x21, starting transfers between devices, send(): return lax.ppermute(x, ('tensor', 'dp'), home_pairs(hops, across))  38.2 us
    another operation x1, loops' own time, special(): lax.switch(index, branches, acts, mine, following, basis_in, basis_out, l...  31 us
    pallas_call x2, Pallas kernels, squares_of_pieces(): pl.pallas_call(functools.partial(pieces_kernel, cap, pairs, first), grid_...  22.7 us
    ppermute x20, waiting for transfers between devices, swap_dp(): return lax.ppermute(x, 'dp', [(d, d ^ k) for d in range(n_dp)])  7.42 us
  transfers between devices with their start and end apart: 41, of which 14 were waited for; matrix products, arithmetic and copies ran while one was open for 4% of the time, Pallas kernels for 18%

commit v1 on v0

--- a/solution.py
+++ b/solution.py
@@ -330,9 +330,11 @@
 
     packed = pack(grads, following, True)
     arrived = [None] * c2
+    last = None
     for i in range(c2 - 1, -1, -1):
-        arrived[i] = to_home(packed[i] if i >= c2 - 2 else tie(packed[i], arrived[c2 - 1]))
-    far_in = swap(tie(basis_in, arrived[c2 - 1]), 2)
+        arrived[i] = to_home(packed[i] if last is None else tie(packed[i], last))
+        last = arrived[i]
+    far_in = swap(tie(basis_in, last), 2)
     near_in = swap(tie(basis_in, arrived[c2 - 1]))
     far_near = swap(far_in)
 
@@ -345,10 +347,7 @@
         blocks[i] = halves(outer, inner)
 
     def product(i):
-        mine, other = blocks[i]
-        if i >= 1:
-            mine = tie(mine, sums[i - 1])
-        given[i], held[i] = products(c, mine, other, basis_out)
+        given[i], held[i] = products(c, *blocks[i], basis_out)
 
     def add_core(i):
         sums[i] = held[i] + swap(given[i]).astype(F32)
@@ -358,24 +357,18 @@
     for i in range(m):
         own[i] = merged(packed, arrived, i)
         v = own[i] if i == 0 else jnp.where(w == 2, fb[i - 1], own[i])
+        fa[i] = send(tie(v, *([held[i - 3]] if i >= 3 else [])), [(0, 1), (1, 2)] + ([(2, 3)] if i else []))
+        m1[i] = send(own[i], [(1, 0)])
+        if i >= 1:
+            meet(i - 1)
+        if i >= 3:
+            add_core(i - 3)
         after = []
         if i >= 2:
             after += blocks[i - 2]
+            product(i - 2)
         if i >= 3:
             after.append(sums[i - 3])
-        fa[i] = send(tie(v, *after), [(0, 1), (1, 2)] + ([(2, 3)] if i else []))
-        m1[i] = send(own[i], [(1, 0)])
-        if i >= 2:
-            blocks[i - 2] = (tie(blocks[i - 2][0], fb[i - 1]), blocks[i - 2][1])
-            product(i - 2)
-            add_core(i - 2)
-        if i >= 1:
-            meet(i - 1)
-        after = []
-        if i >= 2:
-            after.append(held[i - 2])
-        if i >= 3:
-            after.append(fars[i - 3])
         if i == m - 1:
             in_local = project_in(kept, [basis_in, near_in, far_in, far_near], me)
             after.append(in_local)
@@ -388,17 +381,18 @@
     in_arrived = to_home(in_packed)
     in_own = jnp.concatenate([merged(in_packed, in_arrived, i) for i in range(m)], axis=0)
 
-    after = [fb[m - 1], sums[m - 3], blocks[m - 2][1]]
+    after = [fb[m - 1], held[m - 3], fars[m - 4], blocks[m - 2][1]]
     fa[m] = send(tie(fb[m - 1], *after), [(2, 3)])
     r1 = send(tie(in_own, *after), [(0, 1), (1, 2)])
     i1 = send(in_own, [(1, 0)])
+    add_core(m - 3)
     blocks[m - 2] = (tie(blocks[m - 2][0], fb[m - 1]), blocks[m - 2][1])
     product(m - 2)
-    add_core(m - 2)
     meet(m - 1)
     r2 = send(tie(r1, fa[m], fars[m - 3], held[m - 2]), [(1, 2), (2, 3)])
+    add_core(m - 2)
     product(m - 1)
-    r3 = send(tie(r2, fars[m - 2], held[m - 1]), [(2, 3)])
+    r3 = send(tie(r2, sums[m - 2], held[m - 1]), [(2, 3)])
     add_core(m - 1)
     outer = jnp.where(w == 0, in_own, jnp.where(w == 1, r1, jnp.where(w == 2, r2, r3)))
     inner = jnp.where(w == 0, i1, jnp.where(w == 1, in_own, jnp.where(w == 2, r1, r2)))

time: 345 us -> 350 us (1.014); the launches traced: 340 us -> 352 us
  starting transfers between devices: 81 us -> 98.9 us
  waiting for transfers between devices: 120 us -> 104 us
  other arithmetic: 12.5 us -> 26.9 us
  loops' own time: 31 us -> 20.1 us
  matrix products: 3.16 us -> 8.89 us
    ppermute x21, waiting for transfers between devices: 113 us -> 94.6 us  [send(): return lax.ppermute(x, ('tensor', 'dp'), home_pairs(hops, across))]
    ppermute x21, starting transfers between devices: 38.2 us -> 54.3 us  [send(): return lax.ppermute(x, ('tensor', 'dp'), home_pairs(hops, across))]
    another operation x1, loops' own time: 31 us -> 20.1 us  [special(): lax.switch(index, branches, acts, mine, following, basis_in, basis_out, l...]
    dot_general x4, matrix products: 3.16 us -> 8.89 us  [project_in(): t = jnp.dot(a, b, preferred_element_type=F32)]
    select_n x5 -> x4, other arithmetic: 3.34 us -> 7.36 us  [halves(): return (mine, swap(jnp.where(want_outer, inner, outer)))]
  transfers between devices with their start and end apart: 41 -> 41, of which waited for: 14 -> 13; matrix products, arithmetic and copies ran while one was open for 4% -> 11% of each run, Pallas kernels for 18% -> 18%
where the time goes in v1:
time: 350 us; the launch traced here: 352 us
  waiting for transfers between devices  104 us (30%)
  starting transfers between devices  98.9 us (28%)
  Pallas kernels  76.5 us (22%)
  other arithmetic  26.9 us (8%)
  loops' own time  20.1 us (6%)
  matrix products  8.89 us (3%)
  local copies, waits for them, and re-layouts  7.27 us (2%)
  blocking collectives  5.36 us (2%)
  between operations  4.05 us (1%)
    ppermute x21, waiting for transfers between devices, send(): return lax.ppermute(x, ('tensor', 'dp'), home_pairs(hops, across))  94.6 us
    ppermute x21, starting transfers between devices, send(): return lax.ppermute(x, ('tensor', 'dp'), home_pairs(hops, across))  54.3 us
    pallas_call x4, Pallas kernels, products(): pl.pallas_call(product_kernel, grid_spec=pltpu.PrefetchScalarGridSpec(num...  48.6 us
    ppermute x20, starting transfers between devices, swap_dp(): return lax.ppermute(x, 'dp', [(d, d ^ k) for d in range(n_dp)])  44.6 us
    pallas_call x2, Pallas kernels, squares_of_pieces(): pl.pallas_call(functools.partial(pieces_kernel, cap, pairs, first), grid_...  22.6 us
    another operation x1, loops' own time, special(): lax.switch(index, branches, acts, mine, following, basis_in, basis_out, l...  20.1 us
    ppermute x20, waiting for transfers between devices, swap_dp(): return lax.ppermute(x, 'dp', [(d, d ^ k) for d in range(n_dp)])  9.16 us
    dot_general x4, matrix products, project_in(): t = jnp.dot(a, b, preferred_element_type=F32)  8.89 us
  transfers between devices with their start and end apart: 41, of which 13 were waited for; matrix products, arithmetic and copies ran while one was open for 11% of the time, Pallas kernels for 18%

profile of v1, /device:TPU:3, one launch (start us, length us, event | category | flops | bytes accessed | tf_op | source)
XLA Modules:
  0.0 351.7 jit_solution(9486457463719233902)
XLA Ops:
  5.0 5.4 %all-reduce = s32[8]{0:T(128)S(1)} all-reduce(s32[8]{0:T(128)S(1)} %dynamic-update-slice), channel_id=1, replica_groups=mesh['groups'=2,'tensor'=4,'dp'=4] {'groups','dp'}, use_global_device_ids=true, to_apply=%add | all-reduce | flops 8 | bytes 64
  13.6 337.1 %conditional.1 = (bf16[3584,1024]{1,0:T(8,128)(2,1)}) conditional(s32[]{:T(128)} %clamp.3, (s32[8]{0:T(128)S(1)}, bf16[1,288,3584]{2,1,0:T(8,128)(2,1)S(1)}, bf16[288,1792]{1,0:T(8,128)(2,1)S(1)}, bf16[3584,3584]{1,0:T(8,128)(2,1)}, bf16[1,288,4096]{2,1,0:T(8,128)(2,1)}, /*index=5*/bf16[1024,1024]{1,0:T(8,128)(2,1)}, ...), branch_computations={%region_2.3_spmd, %region_3.4_spmd, %region_4.5_spmd, %region_5.6_... | conditional | flops 2471141888 | bytes 369167616 | solution.py:430
  22.6 3.9 %branch_2_fun.8 = (bf16[224,1792]{1,0:T(8,128)(2,1)S(1)}, bf16[224,1792]{1,0:T(8,128)(2,1)S(1)}, bf16[224,1792]{1,0:T(8,128)(2,1)S(1)}) custom-call(s32[4]{0:T(128)S(1)} %dynamic_slice.165.lens_ref, s32[1]{0:T(128)} %bitcast.32.me_ref, bf16[288,1792]{1,0:T(8,128)(2,1)S(1)} %dynamic-slice_bitcast_fusion.2.own_ref, bf16[288,1792]{1,0:T(8,128)(2,1)} %copy-done.6), custom_call_target="tpu_custom_call" | custom-call | flops 1 | bytes 1 | tf_op jit(solution)/shard_map/cond/branch_2_fun/pallas_call | solution.py:135
  28.1 6.5 %collective-permute-start.82 = (bf16[224,1792]{1,0:T(8,128)(2,1)S(1)}, bf16[224,1792]{1,0:T(8,128)(2,1)}, u32[]{:S(2)}, u32[]{:S(2)}) collective-permute-start(bf16[224,1792]{1,0:T(8,128)(2,1)S(1)} %get-tuple-element.140), channel_id=1, source_target_pairs={{2,0},{6,4},{3,1},{7,5},{12,14},{8,10},{13,15},{9,11},{18,16},{22,... | collective-permute-start | bytes 2408456 | tf_op jit(solution)/shard_map/cond/branch_2_fun/ppermute | solution.py:288
  35.9 12.9 %collective-permute-done.82 = bf16[224,1792]{1,0:T(8,128)(2,1)} collective-permute-done((bf16[224,1792]{1,0:T(8,128)(2,1)S(1)}, bf16[224,1792]{1,0:T(8,128)(2,1)}, u32[]{:S(2)}, u32[]{:S(2)}) %collective-permute-start.82) | collective-permute-done | bytes 802848 | tf_op jit(solution)/shard_map/cond/branch_2_fun/ppermute | solution.py:288
  48.8 15.7 %collective-permute-done.81 = bf16[224,1792]{1,0:T(8,128)(2,1)S(1)} collective-permute-done((bf16[224,1792]{1,0:T(8,128)(2,1)}, bf16[224,1792]{1,0:T(8,128)(2,1)S(1)}, u32[]{:S(2)}, u32[]{:S(2)}) %collective-permute-start.81) | collective-permute-done | bytes 802848 | tf_op jit(solution)/shard_map/cond/branch_2_fun/ppermute | solution.py:288
  68.0 6.4 %collective-permute-start.87 = (bf16[224,1792]{1,0:T(8,128)(2,1)S(1)}, bf16[224,1792]{1,0:T(8,128)(2,1)}, u32[]{:S(2)}, u32[]{:S(2)}) collective-permute-start(bf16[224,1792]{1,0:T(8,128)(2,1)S(1)} %get-tuple-element.144), channel_id=1, source_target_pairs={{2,0},{6,4},{3,1},{7,5},{12,14},{8,10},{13,15},{9,11},{18,16},{22,... | collective-permute-start | bytes 2408456 | tf_op jit(solution)/shard_map/cond/branch_2_fun/ppermute | solution.py:288
  76.0 8.5 %collective-permute-done.83 = bf16[224,1792]{1,0:T(8,128)(2,1)} collective-permute-done((bf16[224,1792]{1,0:T(8,128)(2,1)S(1)}, bf16[224,1792]{1,0:T(8,128)(2,1)}, u32[]{:S(2)}, u32[]{:S(2)}) %collective-permute-start.83) | collective-permute-done | bytes 802848 | tf_op jit(solution)/shard_map/cond/branch_2_fun/ppermute | solution.py:288
  86.8 5.1 %collective-permute-start.88 = (bf16[224,1792]{1,0:T(8,128)(2,1)S(1)}, bf16[224,1792]{1,0:T(8,128)(2,1)}, u32[]{:S(2)}, u32[]{:S(2)}) collective-permute-start(bf16[224,1792]{1,0:T(8,128)(2,1)S(1)} %get-tuple-element.145), channel_id=1, source_target_pairs={{2,0},{6,4},{3,1},{7,5},{12,14},{8,10},{13,15},{9,11},{18,16},{22,... | collective-permute-start | bytes 2408456 | tf_op jit(solution)/shard_map/cond/branch_2_fun/ppermute | solution.py:288
  91.9 3.5 broadcast_select_fusion.37
  95.4 5.1 %collective-permute-start.85 = (bf16[224,1792]{1,0:T(8,128)(2,1)}, bf16[224,1792]{1,0:T(8,128)(2,1)S(1)}, u32[]{:S(2)}, u32[]{:S(2)}) collective-permute-start(bf16[224,1792]{1,0:T(8,128)(2,1)} %get-tuple-element.444), channel_id=1, source_target_pairs={{0,1},{1,0},{2,3},{3,2},{4,5},{5,4},{6,7},{7,6},{8,9},{9,8},{10,11... | collective-permute-start | bytes 2408456 | tf_op jit(solution)/shard_map/cond/branch_2_fun/ppermute | solution.py:221
  105.3 5.5 %collective-permute-start.95 = (bf16[1024,1024]{1,0:T(8,128)(2,1)}, bf16[1024,1024]{1,0:T(8,128)(2,1)}, u32[]{:S(2)}, u32[]{:S(2)}) collective-permute-start(bf16[1024,1024]{1,0:T(8,128)(2,1)} %get-tuple-element.151), channel_id=1, source_target_pairs={{0,1},{1,0},{2,3},{3,2},{4,5},{5,4},{6,7},{7,6},{8,9},{9,8},{10,11... | collective-permute-start | bytes 6291464 | tf_op jit(solution)/shard_map/cond/branch_2_fun/ppermute | solution.py:221
  112.1 4.0 %collective-permute-start.96 = (bf16[1024,1024]{1,0:T(8,128)(2,1)}, bf16[1024,1024]{1,0:T(8,128)(2,1)}, u32[]{:S(2)}, u32[]{:S(2)}) collective-permute-start(bf16[1024,1024]{1,0:T(8,128)(2,1)} %get-tuple-element.151), channel_id=1, source_target_pairs={{0,2},{1,3},{2,0},{3,1},{4,6},{5,7},{6,4},{7,5},{8,10},{9,11},{10,... | collective-permute-start | bytes 6291464 | tf_op jit(solution)/shard_map/cond/branch_2_fun/ppermute | solution.py:221
  117.3 2.9 collective-permute-done.90
  126.4 12.1 %branch_2_fun.9 = (bf16[224,1792]{1,0:T(8,128)(2,1)S(1)}, f32[224,1792]{1,0:T(8,128)S(1)}) custom-call(s32[1]{0:T(128)} %bitcast.33.c_ref, bf16[224,1792]{1,0:T(8,128)(2,1)S(1)} %broadcast_select_fusion.38.mine_ref, bf16[224,1792]{1,0:T(8,128)(2,1)S(1)} %collective-permute-done.85.other_ref, bf16[3584,3584]{1,0:T(8,128)(2,1)} %get-tuple-element.292.b_mine_ref.b_other_ref, ...), custom_call_target="tpu_custom_call" | custom-call | flops 1 | bytes 1 | tf_op jit(solution)/shard_map/cond/branch_2_fun/pallas_call | solution.py:74
  138.6 7.3 %collective-permute-start.86 = (bf16[224,1792]{1,0:T(8,128)(2,1)S(1)}, bf16[224,1792]{1,0:T(8,128)(2,1)S(1)}, u32[]{:S(2)}, u32[]{:S(2)}) collective-permute-start(bf16[224,1792]{1,0:T(8,128)(2,1)S(1)} %get-tuple-element.143), channel_id=1, source_target_pairs={{0,1},{1,0},{2,3},{3,2},{4,5},{5,4},{6,7},{7,6},{8,9},{9,8},{10,11... | collective-permute-start | bytes 2408456 | tf_op jit(solution)/shard_map/cond/branch_2_fun/ppermute | solution.py:221
  153.2 9.4 %collective-permute-start.99 = (bf16[224,1792]{1,0:T(8,128)(2,1)}, bf16[224,1792]{1,0:T(8,128)(2,1)}, u32[]{:S(2)}, u32[]{:S(2)}) collective-permute-start(bf16[224,1792]{1,0:T(8,128)(2,1)} %get-tuple-element.442), channel_id=1, source_target_pairs={{0,2},{1,3},{2,0},{3,1},{4,6},{5,7},{6,4},{7,5},{8,10},{9,11},{10,... | collective-permute-start | bytes 2408456 | tf_op jit(solution)/shard_map/cond/branch_2_fun/ppermute | solution.py:221
  165.6 7.2 %collective-permute-done.92 = bf16[224,1792]{1,0:T(8,128)(2,1)} collective-permute-done((bf16[224,1792]{1,0:T(8,128)(2,1)S(1)}, bf16[224,1792]{1,0:T(8,128)(2,1)}, u32[]{:S(2)}, u32[]{:S(2)}) %collective-permute-start.92) | collective-permute-done | bytes 802848 | tf_op jit(solution)/shard_map/cond/branch_2_fun/ppermute | solution.py:288
  178.9 11.4 %collective-permute-start.98 = (bf16[224,1792]{1,0:T(8,128)(2,1)}, bf16[224,1792]{1,0:T(8,128)(2,1)}, u32[]{:S(2)}, u32[]{:S(2)}) collective-permute-start(bf16[224,1792]{1,0:T(8,128)(2,1)} %collective-permute-done.92), channel_id=1, source_target_pairs={{4,8},{8,12},{5,9},{9,13},{10,6},{6,2},{11,7},{7,3},{20,24},{24,28... | collective-permute-start | bytes 2408456 | tf_op jit(solution)/shard_map/cond/branch_2_fun/ppermute | solution.py:288
  190.3 12.6 %branch_2_fun.10 = (bf16[224,1792]{1,0:T(8,128)(2,1)}, f32[224,1792]{1,0:T(8,128)S(1)}) custom-call(s32[1]{0:T(128)} %bitcast.33.c_ref, bf16[224,1792]{1,0:T(8,128)(2,1)S(1)} %broadcast_select_fusion.36.mine_ref, bf16[224,1792]{1,0:T(8,128)(2,1)S(1)} %collective-permute-done.94.other_ref, bf16[3584,3584]{1,0:T(8,128)(2,1)} %get-tuple-element.292.b_mine_ref.b_other_ref, ...), custom_call_target="tpu_custom_call" | custom-call | flops 1 | bytes 1 | tf_op jit(solution)/shard_map/cond/branch_2_fun/pallas_call | solution.py:74
  207.6 6.6 %collective-permute-start.108 = (bf16[3,224,512]{2,1,0:T(8,128)(2,1)S(1)}, bf16[3,224,512]{2,1,0:T(8,128)(2,1)S(1)}, u32[]{:S(2)}, u32[]{:S(2)}) collective-permute-start(bf16[3,224,512]{2,1,0:T(8,128)(2,1)S(1)} %branch_2_fun.12), channel_id=1, source_target_pairs={{2,0},{6,4},{3,1},{7,5},{12,14},{8,10},{13,15},{9,11},{18,16},{22,... | collective-permute-start | bytes 2064392 | tf_op jit(solution)/shard_map/cond/branch_2_fun/ppermute | solution.py:288
  217.6 11.2 %collective-permute-done.108 = bf16[3,224,512]{2,1,0:T(8,128)(2,1)S(1)} collective-permute-done((bf16[3,224,512]{2,1,0:T(8,128)(2,1)S(1)}, bf16[3,224,512]{2,1,0:T(8,128)(2,1)S(1)}, u32[]{:S(2)}, u32[]{:S(2)}) %collective-permute-start.108) | collective-permute-done | bytes 688160 | tf_op jit(solution)/shard_map/cond/branch_2_fun/ppermute | solution.py:288
  229.7 8.2 %collective-permute-done.102 = bf16[224,1792]{1,0:T(8,128)(2,1)S(1)} collective-permute-done((bf16[224,1792]{1,0:T(8,128)(2,1)}, bf16[224,1792]{1,0:T(8,128)(2,1)S(1)}, u32[]{:S(2)}, u32[]{:S(2)}) %collective-permute-start.102) | collective-permute-done | bytes 802848 | tf_op jit(solution)/shard_map/cond/branch_2_fun/ppermute | solution.py:288
  240.9 11.9 %branch_2_fun.13 = (bf16[224,1792]{1,0:T(8,128)(2,1)S(1)}, f32[224,1792]{1,0:T(8,128)S(1)}) custom-call(s32[1]{0:T(128)} %bitcast.33.c_ref, bf16[224,1792]{1,0:T(8,128)(2,1)S(1)} %get-tuple-element.159.mine_ref, bf16[224,1792]{1,0:T(8,128)(2,1)S(1)} %collective-permute-done.101.other_ref, bf16[3584,3584]{1,0:T(8,128)(2,1)} %get-tuple-element.292.b_mine_ref.b_other_ref, ...), custom_call_target="tpu_custom_call" | custom-call | flops 1 | bytes 1 | tf_op jit(solution)/shard_map/cond/branch_2_fun/pallas_call | solution.py:74
  255.1 11.9 %branch_2_fun.11 = (bf16[224,1792]{1,0:T(8,128)(2,1)S(1)}, f32[224,1792]{1,0:T(8,128)S(1)}) custom-call(s32[1]{0:T(128)} %bitcast.33.c_ref, bf16[224,1792]{1,0:T(8,128)(2,1)S(1)} %broadcast_select_fusion.33.mine_ref, bf16[224,1792]{1,0:T(8,128)(2,1)S(1)} %collective-permute-done.104.other_ref, bf16[3584,3584]{1,0:T(8,128)(2,1)} %get-tuple-element.292.b_mine_ref.b_other_ref, ...), custom_call_target="tpu_custom_call" | custom-call | flops 1 | bytes 1 | tf_op jit(solution)/shard_map/cond/branch_2_fun/pallas_call | solution.py:74
  267.7 8.0 %collective-permute-done.112 = bf16[896,512]{1,0:T(8,128)(2,1)S(1)} collective-permute-done((bf16[896,512]{1,0:T(8,128)(2,1)S(1)}, bf16[896,512]{1,0:T(8,128)(2,1)S(1)}, u32[]{:S(2)}, u32[]{:S(2)}) %collective-permute-start.112) | collective-permute-done | bytes 917536 | tf_op jit(solution)/shard_map/cond/branch_2_fun/ppermute | solution.py:288
  278.8 18.0 %collective-permute-done.114 = bf16[896,512]{1,0:T(8,128)(2,1)S(1)} collective-permute-done((bf16[896,512]{1,0:T(8,128)(2,1)S(1)}, bf16[896,512]{1,0:T(8,128)(2,1)S(1)}, u32[]{:S(2)}, u32[]{:S(2)}) %collective-permute-start.114) | collective-permute-done | bytes 917536 | tf_op jit(solution)/shard_map/cond/branch_2_fun/ppermute | solution.py:288
  297.7 3.6 %collective-permute-start.116 = (bf16[896,512]{1,0:T(8,128)(2,1)S(1)}, bf16[896,512]{1,0:T(8,128)(2,1)S(1)}, u32[]{:S(2)}, u32[]{:S(2)}) collective-permute-start(bf16[896,512]{1,0:T(8,128)(2,1)S(1)} %get-tuple-element.428), channel_id=1, source_target_pairs={{0,1},{1,0},{2,3},{3,2},{4,5},{5,4},{6,7},{7,6},{8,9},{9,8},{10,11... | collective-permute-start | bytes 2752520 | tf_op jit(solution)/shard_map/cond/branch_2_fun/ppermute | solution.py:221
  303.5 7.5 %collective-permute-done.106 = bf16[224,1792]{1,0:T(8,128)(2,1)S(1)} collective-permute-done((bf16[224,1792]{1,0:T(8,128)(2,1)S(1)}, bf16[224,1792]{1,0:T(8,128)(2,1)S(1)}, u32[]{:S(2)}, u32[]{:S(2)}) %collective-permute-start.106) | collective-permute-done | bytes 802848 | tf_op jit(solution)/shard_map/cond/branch_2_fun/ppermute | solution.py:221
  312.9 3.6 %collective-permute-start.117 = (bf16[2,224,1792]{2,1,0:T(8,128)(2,1)S(1)}, bf16[2,224,1792]{2,1,0:T(8,128)(2,1)S(1)}, u32[]{:S(2)}, u32[]{:S(2)}) collective-permute-start(bf16[2,224,1792]{2,1,0:T(8,128)(2,1)S(1)} %pad_maximum_fusion.6.refs_0_), channel_id=1, source_target_pairs={{0,1},{1,0},{2,3},{3,2},{4,5},{5,4},{6,7},{7,6},{8,9},{9,8},{10,11... | collective-permute-start | bytes 4816904 | tf_op jit(solution)/shard_map/cond/branch_2_fun/ppermute | solution.py:221
  316.6 11.8 %branch_2_fun.14 = (bf16[3584,1024]{1,0:T(8,128)(2,1)}, bf16[4,288,1024]{2,1,0:T(8,128)(2,1)S(1)}) custom-call(s32[4]{0:T(128)S(1)} %dynamic_slice.165.lens_ref, s32[1]{0:T(128)} %bitcast.32.me_ref, bf16[2,224,1792]{2,1,0:T(8,128)(2,1)S(1)} %pad_maximum_fusion.6.refs_0_, bf16[2,224,1792]{2,1,0:T(8,128)(2,1)S(1)} %pad_maximum_fusion.7.refs_1_, ...), custom_call_target="tpu_custom_call" | custom-call | flops 1 | bytes 1 | tf_op jit(solution)/shard_map/cond/branch_2_fun/pallas_call | solution.py:203
  328.4 10.8 %branch_2_fun.15 = bf16[3584,1024]{1,0:T(8,128)(2,1)} custom-call(s32[4]{0:T(128)S(1)} %dynamic_slice.165.lens_ref, s32[1]{0:T(128)} %bitcast.32.me_ref, bf16[2,224,1792]{2,1,0:T(8,128)(2,1)S(1)} %collective-permute-done.117.refs_0_, bf16[2,224,1792]{2,1,0:T(8,128)(2,1)S(1)} %collective-permute-done.119.refs_1_, ...), custom_call_target="tpu_custom_call", output_to_operand_aliasing={{}: (5, {})} | custom-call | flops 1 | bytes 1 | tf_op jit(solution)/shard_map/cond/branch_2_fun/pallas_call | solution.py:203
  (116 shorter events, 69.1 us)
Async XLA Ops:
  28.1 20.7 %collective-permute-start.82 = (bf16[224,1792]{1,0:T(8,128)(2,1)S(1)}, bf16[224,1792]{1,0:T(8,128)(2,1)}, u32[]{:S(2)}, u32[]{:S(2)}) collective-permute-start(bf16[224,1792]{1,0:T(8,128)(2,1)S(1)} %get-tuple-element.140), channel_id=1, source_target_pairs={{2,0},{6,4},{3,1},{7,5},{12,14},{8,10},{13,15},{9,11},{18,16},{22,... | collective-permute-start | bytes 2408456 | tf_op jit(solution)/shard_map/cond/branch_2_fun/ppermute | solution.py:288
  34.6 29.9 %collective-permute-start.81 = (bf16[224,1792]{1,0:T(8,128)(2,1)}, bf16[224,1792]{1,0:T(8,128)(2,1)S(1)}, u32[]{:S(2)}, u32[]{:S(2)}) collective-permute-start(bf16[224,1792]{1,0:T(8,128)(2,1)} %collective-permute-done.80), channel_id=1, source_target_pairs={{4,8},{8,12},{5,9},{9,13},{10,6},{6,2},{11,7},{7,3},{20,24},{24,28... | collective-permute-start | bytes 2408456 | tf_op jit(solution)/shard_map/cond/branch_2_fun/ppermute | solution.py:288
  66.7 17.8 %collective-permute-start.83 = (bf16[224,1792]{1,0:T(8,128)(2,1)S(1)}, bf16[224,1792]{1,0:T(8,128)(2,1)}, u32[]{:S(2)}, u32[]{:S(2)}) collective-permute-start(bf16[224,1792]{1,0:T(8,128)(2,1)S(1)} %get-tuple-element.447), channel_id=1, source_target_pairs={{0,4},{4,8},{8,12},{1,5},{5,9},{9,13},{14,10},{10,6},{6,2},{15,11}... | collective-permute-start | bytes 2408456 | tf_op jit(solution)/shard_map/cond/branch_2_fun/ppermute | solution.py:288
  68.0 18.8 %collective-permute-start.87 = (bf16[224,1792]{1,0:T(8,128)(2,1)S(1)}, bf16[224,1792]{1,0:T(8,128)(2,1)}, u32[]{:S(2)}, u32[]{:S(2)}) collective-permute-start(bf16[224,1792]{1,0:T(8,128)(2,1)S(1)} %get-tuple-element.144), channel_id=1, source_target_pairs={{2,0},{6,4},{3,1},{7,5},{12,14},{8,10},{13,15},{9,11},{18,16},{22,... | collective-permute-start | bytes 2408456 | tf_op jit(solution)/shard_map/cond/branch_2_fun/ppermute | solution.py:288
  74.4 17.5 %collective-permute-start.84 = (bf16[224,1792]{1,0:T(8,128)(2,1)S(1)}, bf16[224,1792]{1,0:T(8,128)(2,1)}, u32[]{:S(2)}, u32[]{:S(2)}) collective-permute-start(bf16[224,1792]{1,0:T(8,128)(2,1)S(1)} %get-tuple-element.145), channel_id=1, source_target_pairs={{4,0},{5,1},{10,14},{11,15},{20,16},{21,17},{26,30},{27,31}} | collective-permute-start | bytes 2408456 | tf_op jit(solution)/shard_map/cond/branch_2_fun/ppermute | solution.py:288
  84.5 17.1 %collective-permute-start.89 = (bf16[224,1792]{1,0:T(8,128)(2,1)}, bf16[224,1792]{1,0:T(8,128)(2,1)}, u32[]{:S(2)}, u32[]{:S(2)}) collective-permute-start(bf16[224,1792]{1,0:T(8,128)(2,1)} %collective-permute-done.83), channel_id=1, source_target_pairs={{4,8},{8,12},{5,9},{9,13},{10,6},{6,2},{11,7},{7,3},{20,24},{24,28... | collective-permute-start | bytes 2408456 | tf_op jit(solution)/shard_map/cond/branch_2_fun/ppermute | solution.py:288
  86.8 25.3 %collective-permute-start.88 = (bf16[224,1792]{1,0:T(8,128)(2,1)S(1)}, bf16[224,1792]{1,0:T(8,128)(2,1)}, u32[]{:S(2)}, u32[]{:S(2)}) collective-permute-start(bf16[224,1792]{1,0:T(8,128)(2,1)S(1)} %get-tuple-element.145), channel_id=1, source_target_pairs={{2,0},{6,4},{3,1},{7,5},{12,14},{8,10},{13,15},{9,11},{18,16},{22,... | collective-permute-start | bytes 2408456 | tf_op jit(solution)/shard_map/cond/branch_2_fun/ppermute | solution.py:288
  95.4 22.0 %collective-permute-start.85 = (bf16[224,1792]{1,0:T(8,128)(2,1)}, bf16[224,1792]{1,0:T(8,128)(2,1)S(1)}, u32[]{:S(2)}, u32[]{:S(2)}) collective-permute-start(bf16[224,1792]{1,0:T(8,128)(2,1)} %get-tuple-element.444), channel_id=1, source_target_pairs={{0,1},{1,0},{2,3},{3,2},{4,5},{5,4},{6,7},{7,6},{8,9},{9,8},{10,11... | collective-permute-start | bytes 2408456 | tf_op jit(solution)/shard_map/cond/branch_2_fun/ppermute | solution.py:221
  104.0 16.2 %collective-permute-start.90 = (bf16[224,1792]{1,0:T(8,128)(2,1)}, bf16[224,1792]{1,0:T(8,128)(2,1)}, u32[]{:S(2)}, u32[]{:S(2)}) collective-permute-start(bf16[224,1792]{1,0:T(8,128)(2,1)} %get-tuple-element.440), channel_id=1, source_target_pairs={{0,4},{4,8},{8,12},{1,5},{5,9},{9,13},{14,10},{10,6},{6,2},{15,11}... | collective-permute-start | bytes 2408456 | tf_op jit(solution)/shard_map/cond/branch_2_fun/ppermute | solution.py:288
  105.3 40.6 %collective-permute-start.95 = (bf16[1024,1024]{1,0:T(8,128)(2,1)}, bf16[1024,1024]{1,0:T(8,128)(2,1)}, u32[]{:S(2)}, u32[]{:S(2)}) collective-permute-start(bf16[1024,1024]{1,0:T(8,128)(2,1)} %get-tuple-element.151), channel_id=1, source_target_pairs={{0,1},{1,0},{2,3},{3,2},{4,5},{5,4},{6,7},{7,6},{8,9},{9,8},{10,11... | collective-permute-start | bytes 6291464 | tf_op jit(solution)/shard_map/cond/branch_2_fun/ppermute | solution.py:221
  112.1 50.4 %collective-permute-start.96 = (bf16[1024,1024]{1,0:T(8,128)(2,1)}, bf16[1024,1024]{1,0:T(8,128)(2,1)}, u32[]{:S(2)}, u32[]{:S(2)}) collective-permute-start(bf16[1024,1024]{1,0:T(8,128)(2,1)} %get-tuple-element.151), channel_id=1, source_target_pairs={{0,2},{1,3},{2,0},{3,1},{4,6},{5,7},{6,4},{7,5},{8,10},{9,11},{10,... | collective-permute-start | bytes 6291464 | tf_op jit(solution)/shard_map/cond/branch_2_fun/ppermute | solution.py:221
  120.2 28.8 %collective-permute-start.91 = (bf16[224,1792]{1,0:T(8,128)(2,1)}, bf16[224,1792]{1,0:T(8,128)(2,1)}, u32[]{:S(2)}, u32[]{:S(2)}) collective-permute-start(bf16[224,1792]{1,0:T(8,128)(2,1)} %collective-permute-done.90), channel_id=1, source_target_pairs={{4,8},{8,12},{5,9},{9,13},{10,6},{6,2},{11,7},{7,3},{20,24},{24,28... | collective-permute-start | bytes 2408456 | tf_op jit(solution)/shard_map/cond/branch_2_fun/ppermute | solution.py:288
  125.7 39.8 %collective-permute-start.93 = (bf16[224,1792]{1,0:T(8,128)(2,1)S(1)}, bf16[224,1792]{1,0:T(8,128)(2,1)S(1)}, u32[]{:S(2)}, u32[]{:S(2)}) collective-permute-start(bf16[224,1792]{1,0:T(8,128)(2,1)S(1)} %get-tuple-element.448), channel_id=1, source_target_pairs={{4,0},{5,1},{10,14},{11,15},{20,16},{21,17},{26,30},{27,31}} | collective-permute-start | bytes 2408456 | tf_op jit(solution)/shard_map/cond/branch_2_fun/ppermute | solution.py:288
  148.2 17.3 %collective-permute-start.100 = (bf16[224,1792]{1,0:T(8,128)(2,1)S(1)}, bf16[224,1792]{1,0:T(8,128)(2,1)S(1)}, u32[]{:S(2)}, u32[]{:S(2)}) collective-permute-start(bf16[224,1792]{1,0:T(8,128)(2,1)S(1)} %copy-done.21), channel_id=1, source_target_pairs={{4,0},{5,1},{10,14},{11,15},{20,16},{21,17},{26,30},{27,31}} | collective-permute-start | bytes 2408456 | tf_op jit(solution)/shard_map/cond/branch_2_fun/ppermute | solution.py:288
  150.2 22.5 %collective-permute-start.92 = (bf16[224,1792]{1,0:T(8,128)(2,1)S(1)}, bf16[224,1792]{1,0:T(8,128)(2,1)}, u32[]{:S(2)}, u32[]{:S(2)}) collective-permute-start(bf16[224,1792]{1,0:T(8,128)(2,1)S(1)} %broadcast_select_fusion.28), channel_id=1, source_target_pairs={{0,4},{4,8},{8,12},{1,5},{5,9},{9,13},{14,10},{10,6},{6,2},{15,11}... | collective-permute-start | bytes 2408456 | tf_op jit(solution)/shard_map/cond/branch_2_fun/ppermute | solution.py:288
  153.2 61.0 %collective-permute-start.99 = (bf16[224,1792]{1,0:T(8,128)(2,1)}, bf16[224,1792]{1,0:T(8,128)(2,1)}, u32[]{:S(2)}, u32[]{:S(2)}) collective-permute-start(bf16[224,1792]{1,0:T(8,128)(2,1)} %get-tuple-element.442), channel_id=1, source_target_pairs={{0,2},{1,3},{2,0},{3,1},{4,6},{5,7},{6,4},{7,5},{8,10},{9,11},{10,... | collective-permute-start | bytes 2408456 | tf_op jit(solution)/shard_map/cond/branch_2_fun/ppermute | solution.py:221
  162.5 14.7 %collective-permute-start.97 = (bf16[1024,1024]{1,0:T(8,128)(2,1)}, bf16[1024,1024]{1,0:T(8,128)(2,1)S(1)}, u32[]{:S(2)}, u32[]{:S(2)}) collective-permute-start(bf16[1024,1024]{1,0:T(8,128)(2,1)} %collective-permute-done.96), channel_id=1, source_target_pairs={{0,1},{1,0},{2,3},{3,2},{4,5},{5,4},{6,7},{7,6},{8,9},{9,8},{10,11... | collective-permute-start | bytes 6291464 | tf_op jit(solution)/shard_map/cond/branch_2_fun/ppermute | solution.py:221
  177.2 37.7 %collective-permute-start.101 = (bf16[224,1792]{1,0:T(8,128)(2,1)}, bf16[224,1792]{1,0:T(8,128)(2,1)S(1)}, u32[]{:S(2)}, u32[]{:S(2)}) collective-permute-start(bf16[224,1792]{1,0:T(8,128)(2,1)} %broadcast_select_fusion.34), channel_id=1, source_target_pairs={{0,1},{1,0},{2,3},{3,2},{4,5},{5,4},{6,7},{7,6},{8,9},{9,8},{10,11... | collective-permute-start | bytes 2408456 | tf_op jit(solution)/shard_map/cond/branch_2_fun/ppermute | solution.py:221
  178.9 36.0 %collective-permute-start.98 = (bf16[224,1792]{1,0:T(8,128)(2,1)}, bf16[224,1792]{1,0:T(8,128)(2,1)}, u32[]{:S(2)}, u32[]{:S(2)}) collective-permute-start(bf16[224,1792]{1,0:T(8,128)(2,1)} %collective-permute-done.92), channel_id=1, source_target_pairs={{4,8},{8,12},{5,9},{9,13},{10,6},{6,2},{11,7},{7,3},{20,24},{24,28... | collective-permute-start | bytes 2408456 | tf_op jit(solution)/shard_map/cond/branch_2_fun/ppermute | solution.py:288
  207.6 21.2 %collective-permute-start.108 = (bf16[3,224,512]{2,1,0:T(8,128)(2,1)S(1)}, bf16[3,224,512]{2,1,0:T(8,128)(2,1)S(1)}, u32[]{:S(2)}, u32[]{:S(2)}) collective-permute-start(bf16[3,224,512]{2,1,0:T(8,128)(2,1)S(1)} %branch_2_fun.12), channel_id=1, source_target_pairs={{2,0},{6,4},{3,1},{7,5},{12,14},{8,10},{13,15},{9,11},{18,16},{22,... | collective-permute-start | bytes 2064392 | tf_op jit(solution)/shard_map/cond/branch_2_fun/ppermute | solution.py:288
  214.1 15.5 %collective-permute-start.103 = (bf16[224,1792]{1,0:T(8,128)(2,1)}, bf16[224,1792]{1,0:T(8,128)(2,1)S(1)}, u32[]{:S(2)}, u32[]{:S(2)}) collective-permute-start(bf16[224,1792]{1,0:T(8,128)(2,1)} %collective-permute-done.88), channel_id=1, source_target_pairs={{4,0},{5,1},{10,14},{11,15},{20,16},{21,17},{26,30},{27,31}} | collective-permute-start | bytes 2408456 | tf_op jit(solution)/shard_map/cond/branch_2_fun/ppermute | solution.py:288
  214.9 23.0 %collective-permute-start.102 = (bf16[224,1792]{1,0:T(8,128)(2,1)}, bf16[224,1792]{1,0:T(8,128)(2,1)S(1)}, u32[]{:S(2)}, u32[]{:S(2)}) collective-permute-start(bf16[224,1792]{1,0:T(8,128)(2,1)} %collective-permute-done.98), channel_id=1, source_target_pairs={{8,12},{9,13},{6,2},{7,3},{24,28},{25,29},{22,18},{23,19}} | collective-permute-start | bytes 2408456 | tf_op jit(solution)/shard_map/cond/branch_2_fun/ppermute | solution.py:288
  217.5 36.2 %collective-permute-start.111 = (bf16[224,1792]{1,0:T(8,128)(2,1)S(1)}, bf16[224,1792]{1,0:T(8,128)(2,1)S(1)}, u32[]{:S(2)}, u32[]{:S(2)}) collective-permute-start(bf16[224,1792]{1,0:T(8,128)(2,1)S(1)} %fusion.52), channel_id=1, source_target_pairs={{0,2},{1,3},{2,0},{3,1},{4,6},{5,7},{6,4},{7,5},{8,10},{9,11},{10,... | collective-permute-start | bytes 2408456 | tf_op jit(solution)/shard_map/cond/branch_2_fun/ppermute | solution.py:221
  228.9 24.8 %collective-permute-start.109 = (bf16[896,512]{1,0:T(8,128)(2,1)S(1)}, bf16[896,512]{1,0:T(8,128)(2,1)S(1)}, u32[]{:S(2)}, u32[]{:S(2)}) collective-permute-start(bf16[896,512]{1,0:T(8,128)(2,1)S(1)} %pad_maximum_fusion.8), channel_id=1, source_target_pairs={{0,4},{4,8},{1,5},{5,9},{14,10},{10,6},{15,11},{11,7},{16,20},{20,... | collective-permute-start | bytes 2752520 | tf_op jit(solution)/shard_map/cond/branch_2_fun/ppermute | solution.py:288
  239.9 15.3 %collective-permute-start.104 = (bf16[224,1792]{1,0:T(8,128)(2,1)S(1)}, bf16[224,1792]{1,0:T(8,128)(2,1)S(1)}, u32[]{:S(2)}, u32[]{:S(2)}) collective-permute-start(bf16[224,1792]{1,0:T(8,128)(2,1)S(1)} %get-tuple-element.434), channel_id=1, source_target_pairs={{0,1},{1,0},{2,3},{3,2},{4,5},{5,4},{6,7},{7,6},{8,9},{9,8},{10,11... | collective-permute-start | bytes 2408456 | tf_op jit(solution)/shard_map/cond/branch_2_fun/ppermute | solution.py:221
  253.0 25.8 %collective-permute-start.115 = (bf16[896,512]{1,0:T(8,128)(2,1)S(1)}, bf16[896,512]{1,0:T(8,128)(2,1)S(1)}, u32[]{:S(2)}, u32[]{:S(2)}) collective-permute-start(bf16[896,512]{1,0:T(8,128)(2,1)S(1)} %pad_maximum_fusion.8), channel_id=1, source_target_pairs={{4,0},{5,1},{10,14},{11,15},{20,16},{21,17},{26,30},{27,31}} | collective-permute-start | bytes 2752520 | tf_op jit(solution)/shard_map/cond/branch_2_fun/ppermute | solution.py:288
  253.7 22.0 %collective-permute-start.112 = (bf16[896,512]{1,0:T(8,128)(2,1)S(1)}, bf16[896,512]{1,0:T(8,128)(2,1)S(1)}, u32[]{:S(2)}, u32[]{:S(2)}) collective-permute-start(bf16[896,512]{1,0:T(8,128)(2,1)S(1)} %collective-permute-done.109), channel_id=1, source_target_pairs={{4,8},{8,12},{5,9},{9,13},{10,6},{6,2},{11,7},{7,3},{20,24},{24,28... | collective-permute-start | bytes 2752520 | tf_op jit(solution)/shard_map/cond/branch_2_fun/ppermute | solution.py:288
  275.7 21.1 %collective-permute-start.114 = (bf16[896,512]{1,0:T(8,128)(2,1)S(1)}, bf16[896,512]{1,0:T(8,128)(2,1)S(1)}, u32[]{:S(2)}, u32[]{:S(2)}) collective-permute-start(bf16[896,512]{1,0:T(8,128)(2,1)S(1)} %collective-permute-done.112), channel_id=1, source_target_pairs={{8,12},{9,13},{6,2},{7,3},{24,28},{25,29},{22,18},{23,19}} | collective-permute-start | bytes 2752520 | tf_op jit(solution)/shard_map/cond/branch_2_fun/ppermute | solution.py:288
  277.0 24.3 %collective-permute-start.118 = (bf16[224,1792]{1,0:T(8,128)(2,1)S(1)}, bf16[224,1792]{1,0:T(8,128)(2,1)S(1)}, u32[]{:S(2)}, u32[]{:S(2)}) collective-permute-start(bf16[224,1792]{1,0:T(8,128)(2,1)S(1)} %get-tuple-element.426), channel_id=1, source_target_pairs={{0,2},{1,3},{2,0},{3,1},{4,6},{5,7},{6,4},{7,5},{8,10},{9,11},{10,... | collective-permute-start | bytes 2408456 | tf_op jit(solution)/shard_map/cond/branch_2_fun/ppermute | solution.py:221
  277.3 33.7 %collective-permute-start.106 = (bf16[224,1792]{1,0:T(8,128)(2,1)S(1)}, bf16[224,1792]{1,0:T(8,128)(2,1)S(1)}, u32[]{:S(2)}, u32[]{:S(2)}) collective-permute-start(bf16[224,1792]{1,0:T(8,128)(2,1)S(1)} %fusion.51), channel_id=1, source_target_pairs={{0,2},{1,3},{2,0},{3,1},{4,6},{5,7},{6,4},{7,5},{8,10},{9,11},{10,... | collective-permute-start | bytes 2408456 | tf_op jit(solution)/shard_map/cond/branch_2_fun/ppermute | solution.py:221
  303.3 25.1 %collective-permute-start.119 = (bf16[2,224,1792]{2,1,0:T(8,128)(2,1)S(1)}, bf16[2,224,1792]{2,1,0:T(8,128)(2,1)S(1)}, u32[]{:S(2)}, u32[]{:S(2)}) collective-permute-start(bf16[2,224,1792]{2,1,0:T(8,128)(2,1)S(1)} %pad_maximum_fusion.7.refs_1_), channel_id=1, source_target_pairs={{0,1},{1,0},{2,3},{3,2},{4,5},{5,4},{6,7},{7,6},{8,9},{9,8},{10,11... | collective-permute-start | bytes 4816904 | tf_op jit(solution)/shard_map/cond/branch_2_fun/ppermute | solution.py:221
  312.9 15.5 %collective-permute-start.117 = (bf16[2,224,1792]{2,1,0:T(8,128)(2,1)S(1)}, bf16[2,224,1792]{2,1,0:T(8,128)(2,1)S(1)}, u32[]{:S(2)}, u32[]{:S(2)}) collective-permute-start(bf16[2,224,1792]{2,1,0:T(8,128)(2,1)S(1)} %pad_maximum_fusion.6.refs_0_), channel_id=1, source_target_pairs={{0,1},{1,0},{2,3},{3,2},{4,5},{5,4},{6,7},{7,6},{8,9},{9,8},{10,11... | collective-permute-start | bytes 4816904 | tf_op jit(solution)/shard_map/cond/branch_2_fun/ppermute | solution.py:221
  (17 other events, 155.4 us)
